TPU v7x, 128 devices: a whole 4x4x4 slice. The times are simulated.
128 devices in a mesh: ctx: 16 (over y, z), tp: 8 (over x, core).
Axes of the slice: x: 4, y: 4, z: 4, core: 2. Of those that a mesh axis runs over, the one named last changes fastest.
Arguments:
- query_proj: bfloat16 [8192, 8192], P('ctx', 'tp'), may hold values from -6 to 6
- key_proj: bfloat16 [8192, 8192], P('ctx', 'tp'), may hold values from -6 to 6
- value_proj: bfloat16 [8192, 8192], P('ctx', 'tp'), may hold values from -6 to 6
- filter_spectrum: bfloat16 [2, 16384, 8192], P(None, 'ctx', 'tp'), may hold values from -24 to 24
- skip_gain: float32 [8192], P('tp'), may hold values from 0.5 to 1.5
- out_weight: bfloat16 [8192, 8192], P('tp'), may hold values from -0.09375 to 0.09375
Outputs:
- block_out: bfloat16 [8192, 8192], P('ctx', 'tp')
All inputs are finite; a program needn't handle non-finite values.
Results may differ from a plain program's by a relative error of at most 0.012.
Values may be sent and summed in bfloat16 or wider, within the bound.
No kernel may reach another device: no remote copies, remote signals or barrier semaphores. Data moves between devices by JAX's collectives and lax.ppermute only.
A program may use at most 128 MiB of HBM per device.

v0:
```python
import math

import jax
import jax.numpy as jnp
from jax import lax
from jax.sharding import PartitionSpec as P

FFT_COLS = 128


circle = 2.0 * math.pi
highest = lax.Precision.HIGHEST


def table(first, second, period):
    left = lax.broadcasted_iota(jnp.int32, (first, second), 0)
    right = lax.broadcasted_iota(jnp.int32, (first, second), 1)
    angle = (left * right % period).astype(jnp.float32) * (circle / period)
    return (jnp.cos(angle), jnp.sin(angle))


def twiddle(left_ids, right_ids, period):
    angle = (left_ids[:, None] * right_ids[None, :] % period).astype(jnp.float32) * (
        circle / period
    )
    return (jnp.cos(angle)[:, :, None], jnp.sin(angle)[:, :, None])


def split_table(values):
    high_part = values.astype(jnp.bfloat16)
    low_part = (values - high_part.astype(jnp.float32)).astype(jnp.bfloat16)
    return (high_part, low_part)


def forward_rows(signal, col_ids, fft_len):
    half_rows = signal.shape[0]
    fft_rows = 2 * half_rows
    cos_rows, sin_rows = table(fft_rows, half_rows, fft_rows)
    cos_high, cos_low = split_table(cos_rows)
    sin_high, sin_low = split_table(sin_rows)
    stacked = jnp.concatenate([cos_high, cos_low, sin_high, sin_low], axis=0)
    products = jnp.einsum("kn,nic->kic", stacked, signal, preferred_element_type=jnp.float32)
    real_part = products[:fft_rows] + products[fft_rows : 2 * fft_rows]
    imag_part = -(products[2 * fft_rows : 3 * fft_rows] + products[3 * fft_rows :])
    tw_cos, tw_sin = twiddle(jnp.arange(fft_rows, dtype=jnp.int32), col_ids, fft_len)
    return (real_part * tw_cos + imag_part * tw_sin, imag_part * tw_cos - real_part * tw_sin)


def middle(real_in, imag_in, spec_real, spec_imag, row_ids, fft_len):
    cos_cols, sin_cols = table(FFT_COLS, FFT_COLS, FFT_COLS)
    zr = jnp.einsum("kn,mnc->kmc", cos_cols, real_in, precision=highest) + jnp.einsum(
        "kn,mnc->kmc", sin_cols, imag_in, precision=highest
    )
    zi = jnp.einsum("kn,mnc->kmc", cos_cols, imag_in, precision=highest) - jnp.einsum(
        "kn,mnc->kmc", sin_cols, real_in, precision=highest
    )
    prod_real = zr * spec_real - zi * spec_imag
    prod_imag = zr * spec_imag + zi * spec_real
    ur = jnp.einsum("nk,kmc->nmc", cos_cols, prod_real, precision=highest) - jnp.einsum(
        "nk,kmc->nmc", sin_cols, prod_imag, precision=highest
    )
    ui = jnp.einsum("nk,kmc->nmc", cos_cols, prod_imag, precision=highest) + jnp.einsum(
        "nk,kmc->nmc", sin_cols, prod_real, precision=highest
    )
    tw_cos, tw_sin = twiddle(jnp.arange(FFT_COLS, dtype=jnp.int32), row_ids, fft_len)
    return (ur * tw_cos - ui * tw_sin, ui * tw_cos + ur * tw_sin)


def inverse_rows(real_in, imag_in, fft_len):
    fft_rows = real_in.shape[1]
    half_rows = fft_rows // 2
    cos_back, sin_back = table(half_rows, fft_rows, fft_rows)
    result = jnp.einsum("mk,ikc->mic", cos_back, real_in, precision=highest) - jnp.einsum(
        "mk,ikc->mic", sin_back, imag_in, precision=highest
    )
    return result * (1.0 / fft_len)


def per_device(query_proj, key_proj, value_proj, filter_spectrum, skip_gain, out_weight):
    signal = (key_proj.astype(jnp.float32) * value_proj.astype(jnp.float32)).astype(jnp.bfloat16)
    tokens, channels = signal.shape
    groups = lax.axis_size("ctx")
    seq_len = tokens * groups
    fft_len = 2 * seq_len
    fft_rows = fft_len // FFT_COLS
    position = lax.axis_index("ctx")
    local = signal.reshape(tokens // FFT_COLS, FFT_COLS, channels)
    moved = lax.all_to_all(local, "ctx", split_axis=1, concat_axis=0, tiled=True)
    spec_parts = filter_spectrum.reshape(2, FFT_COLS // groups, fft_rows, channels)
    spec_rows = lax.all_to_all(spec_parts, "ctx", split_axis=2, concat_axis=1, tiled=True)
    col_ids = position * (FFT_COLS // groups) + jnp.arange(FFT_COLS // groups, dtype=jnp.int32)
    row_ids = position * (fft_rows // groups) + jnp.arange(fft_rows // groups, dtype=jnp.int32)
    real_a, imag_a = forward_rows(moved, col_ids, fft_len)
    real_b, imag_b = (
        lax.all_to_all(real_a, "ctx", split_axis=0, concat_axis=1, tiled=True),
        lax.all_to_all(imag_a, "ctx", split_axis=0, concat_axis=1, tiled=True),
    )
    real_c, imag_c = middle(
        real_b,
        imag_b,
        spec_rows[0].astype(jnp.float32),
        spec_rows[1].astype(jnp.float32),
        row_ids,
        fft_len,
    )
    real_d, imag_d = (
        lax.all_to_all(real_c, "ctx", split_axis=0, concat_axis=1, tiled=True),
        lax.all_to_all(imag_c, "ctx", split_axis=0, concat_axis=1, tiled=True),
    )
    filtered_cols = inverse_rows(real_d, imag_d, fft_len).astype(jnp.bfloat16)
    filtered = lax.all_to_all(
        filtered_cols, "ctx", split_axis=0, concat_axis=1, tiled=True
    ).reshape(tokens, channels)
    gated = (
        query_proj.astype(jnp.float32)
        * (filtered.astype(jnp.float32) + skip_gain * signal.astype(jnp.float32))
    ).astype(jnp.bfloat16)
    terms = jnp.dot(gated, out_weight, preferred_element_type=jnp.float32)
    return lax.psum_scatter(terms, "tp", scatter_dimension=1, tiled=True).astype(jnp.bfloat16)


def solution(mesh):
    in_specs = (
        P("ctx", "tp"),
        P("ctx", "tp"),
        P("ctx", "tp"),
        P(None, "ctx", "tp"),
        P("tp"),
        P("tp", None),
    )
    out_specs = P("ctx", "tp")
    return jax.shard_map(
        per_device, mesh=mesh, in_specs=in_specs, out_specs=out_specs, check_vma=False
    )
```

profile of v0, /device:TPU:0, one launch (start us, length us, event | category | flops | bytes accessed | tf_op | source)
XLA Modules:
  0.0 513.7 jit_solution(8873189976451498246)
XLA Ops:
  6.5 1.9 multiply_convert_fusion.1
  8.5 1.8 copy.35
  10.3 8.1 %all-to-all-start = ((bf16[4,128,1024]{2,0,1:T(4,128)(2,1)}), bf16[4,128,1024]{2,0,1:T(4,128)(2,1)S(1)}, u32[]{:S(2)}, u32[]{:S(2)}) async-start(bf16[4,128,1024]{2,0,1:T(4,128)(2,1)} %copy.35), calls=%async_computation | async-start | bytes 2097152 | tf_op jit(solution)/shard_map/all_to_all | solution.py:88
  18.4 6.5 %copy.42 = bf16[2,8,128,1024]{3,1,0,2:T(8,128)(2,1)} copy(bf16[2,8,128,1024]{3,2,1,0:T(8,128)(2,1)} %bitcast.115) | data formatting | bytes 8388608 | tf_op jit(solution)/shard_map/reshape | solution.py:89
  24.9 11.2 %all-to-all-done = bf16[4,128,1024]{2,0,1:T(4,128)(2,1)S(1)} async-done(((bf16[4,128,1024]{2,0,1:T(4,128)(2,1)}), bf16[4,128,1024]{2,0,1:T(4,128)(2,1)S(1)}, u32[]{:S(2)}, u32[]{:S(2)}) %all-to-all-start) | async-done | bytes 1048608 | tf_op jit(solution)/shard_map/all_to_all | solution.py:88
  36.1 4.6 all-to-all-start.3
  40.7 0.2 subtract_convert_fusion
  40.8 0.1 fusion.82
  41.0 0.1 fusion.93
  41.1 0.3 copy.91
  41.4 1.8 copy.37
  43.2 1.3 all_to_all.86
  44.6 2.4 fusion.34
  46.9 2.8 multiply_subtract_fusion.1
  49.7 4.4 copy.38
  54.0 39.4 %all-to-all-done.3 = bf16[2,8,128,1024]{3,1,0,2:T(8,128)(2,1)} async-done(((bf16[2,8,128,1024]{3,1,0,2:T(8,128)(2,1)}), bf16[2,8,128,1024]{3,1,0,2:T(8,128)(2,1)}, u32[]{:S(2)}, u32[]{:S(2)}) %all-to-all-start.3) | async-done | bytes 4194336 | tf_op jit(solution)/shard_map/all_to_all | solution.py:90
  93.4 4.8 all-to-all-start.1
  98.2 6.6 %copy.40 = f32[128,8,1024]{2,1,0:T(8,128)} copy(f32[128,8,1024]{2,0,1:T(8,128)} %get-tuple-element.5) | data formatting | bytes 8388608 | tf_op jit(solution)/shard_map/sub | solution.py:46
  104.8 43.1 %all-to-all-done.1 = f32[128,8,1024]{2,1,0:T(8,128)} async-done(((f32[128,8,1024]{2,1,0:T(8,128)}), f32[128,8,1024]{2,1,0:T(8,128)}, u32[]{:S(2)}, u32[]{:S(2)}) %all-to-all-start.1) | async-done | bytes 4194336 | tf_op jit(solution)/shard_map/all_to_all | solution.py:95
  148.0 7.0 %all-to-all-start.2 = ((f32[128,8,1024]{2,1,0:T(8,128)}), f32[128,8,1024]{2,1,0:T(8,128)}, u32[]{:S(2)}, u32[]{:S(2)}) async-start(f32[128,8,1024]{2,1,0:T(8,128)} %copy.40), calls=%async_computation.2 | async-start | bytes 8388608 | tf_op jit(solution)/shard_map/all_to_all | solution.py:96
  155.0 4.5 copy.90
  159.5 4.2 slice_convert_fusion.1
  163.8 8.1 %fusion.7 = f32[128,8,1024]{2,0,1:T(8,128)} fusion(f32[16,8,8,1024]{3,2,1,0:T(8,128)} %bitcast.6), kind=kOutput, calls=%fused_computation.11 | convolution fusion | flops 1610842112 | bytes 8388608 | tf_op jit(solution)/shard_map/kn,mnc->kmc/dot_general | solution.py:54
  171.9 8.1 %fusion.9 = f32[128,8,1024]{2,0,1:T(8,128)} fusion(f32[16,8,8,1024]{3,2,1,0:T(8,128)} %bitcast.6), kind=kOutput, calls=%fused_computation.13 | convolution fusion | flops 1610842112 | bytes 8388608 | tf_op jit(solution)/shard_map/kn,mnc->kmc/dot_general | solution.py:51
  180.0 26.3 %all-to-all-done.2 = f32[128,8,1024]{2,1,0:T(8,128)} async-done(((f32[128,8,1024]{2,1,0:T(8,128)}), f32[128,8,1024]{2,1,0:T(8,128)}, u32[]{:S(2)}, u32[]{:S(2)}) %all-to-all-start.2) | async-done | bytes 4194336 | tf_op jit(solution)/shard_map/all_to_all | solution.py:96
  206.3 0.0 copy-start
  206.3 0.0 copy-start.1
  206.3 16.7 %fusion.24 = f32[128,8,1024]{2,0,1:T(8,128)S(1)} fusion(f32[128,8,1024]{2,0,1:T(8,128)} %fusion.7, f32[16,8,8,1024]{3,2,1,0:T(8,128)} %bitcast.10), kind=kOutput, calls=%fused_computation.33 | convolution fusion | flops 1611890688 | bytes 12582912 | tf_op jit(solution)/shard_map/kn,mnc->kmc/dot_general | solution.py:54
  223.0 0.0 copy-done
  223.0 0.0 copy-done.1
  223.0 12.7 %fusion.6 = (f32[128,8,1024]{2,0,1:T(8,128)S(1)}, f32[128,8,1024]{2,0,1:T(8,128)S(1)}) fusion(f32[128,8,1024]{2,0,1:T(8,128)S(1)} %fusion.24, f32[1,16,8,8,1024]{4,3,1,2,0:T(8,128)S(1)} %copy-done.1, f32[1,16,8,8,1024]{4,3,1,2,0:T(8,128)S(1)} %copy-done, f32[128,8,1024]{2,0,1:T(8,128)} %fusion.9, f32[16,8,8,1024]{3,2,1,0:T(8,128)} %bitcast.10), kind=kOutput, calls=%fused_computation.10 | convolution fusion | flops 1618182144 | bytes 29360128 | tf_op jit(solution)/shard_map/kn,mnc->kmc/dot_general | solution.py:51
  235.7 4.0 fusion.47
  239.7 4.3 fusion.45
  244.0 4.8 convolution_subtract_fusion
  248.8 6.8 %multiply_subtract_fusion = (f32[128,8,1024]{2,0,1:T(8,128)}, f32[128,8,1024]{2,0,1:T(8,128)S(1)}) fusion(f32[128,8,1024]{2,0,1:T(8,128)S(1)} %convolution_subtract_fusion, f32[128,8]{0,1:T(8,128)S(1)} %get-tuple-element.14, f32[128,8]{0,1:T(8,128)S(1)} %get-tuple-element.13, f32[128,8,1024]{2,0,1:T(8,128)S(1)} %fusion.45, ...), kind=kOutput, calls=%fused_computation.25 | convolution fusion | flops 1618182144 | bytes 20979712 | tf_op jit(solution)/shard_map/nk,kmc->nmc/dot_general | solution.py:62
  255.5 4.4 copy.48
  259.9 5.3 %all-to-all-start.5 = ((f32[128,8,1024]{2,1,0:T(8,128)}), f32[128,8,1024]{2,1,0:T(8,128)}, u32[]{:S(2)}, u32[]{:S(2)}) async-start(f32[128,8,1024]{2,1,0:T(8,128)} %copy.48), calls=%async_computation.5 | async-start | bytes 8388608 | tf_op jit(solution)/shard_map/all_to_all | solution.py:108
  265.2 6.6 %copy.46 = f32[128,8,1024]{2,1,0:T(8,128)} copy(f32[128,8,1024]{2,0,1:T(8,128)} %get-tuple-element.9) | data formatting | bytes 8388608 | tf_op jit(solution)/shard_map/sub | solution.py:66
  271.8 44.2 %all-to-all-done.5 = f32[128,8,1024]{2,1,0:T(8,128)} async-done(((f32[128,8,1024]{2,1,0:T(8,128)}), f32[128,8,1024]{2,1,0:T(8,128)}, u32[]{:S(2)}, u32[]{:S(2)}) %all-to-all-start.5) | async-done | bytes 4194336 | tf_op jit(solution)/shard_map/all_to_all | solution.py:108
  316.0 5.7 %all-to-all-start.4 = ((f32[128,8,1024]{2,1,0:T(8,128)}), f32[128,8,1024]{2,1,0:T(8,128)}, u32[]{:S(2)}, u32[]{:S(2)}) async-start(f32[128,8,1024]{2,1,0:T(8,128)} %copy.46), calls=%async_computation.4 | async-start | bytes 8388608 | tf_op jit(solution)/shard_map/all_to_all | solution.py:107
  321.7 0.2 reduce-scatter.2.cloned.1.call-start
  321.9 5.9 %fusion.1 = f32[64,8,1024]{2,0,1:T(8,128)} fusion(f32[16,8,8,1024]{3,2,1,0:T(8,128)} %bitcast.25), kind=kOutput, calls=%fused_computation.3 | convolution fusion | flops 805421056 | bytes 6291456 | tf_op jit(solution)/shard_map/mk,ikc->mic/dot_general | solution.py:73
  327.8 45.5 %all-to-all-done.4 = f32[128,8,1024]{2,1,0:T(8,128)} async-done(((f32[128,8,1024]{2,1,0:T(8,128)}), f32[128,8,1024]{2,1,0:T(8,128)}, u32[]{:S(2)}, u32[]{:S(2)}) %all-to-all-start.4) | async-done | bytes 4194336 | tf_op jit(solution)/shard_map/all_to_all | solution.py:107
  373.3 5.3 %multiply_convert_fusion = bf16[64,8,1024]{2,0,1:T(8,128)(2,1)S(1)} fusion(f32[64,8,1024]{2,0,1:T(8,128)} %fusion.1, f32[16,8,8,1024]{3,2,1,0:T(8,128)} %bitcast.21), kind=kOutput, calls=%fused_computation.41 | convolution fusion | flops 806993920 | bytes 7340032 | tf_op jit(solution)/shard_map/mk,ikc->mic/dot_general | solution.py:73
  378.6 0.0 copy-start.2
  378.7 0.0 copy-start.3
  378.7 0.6 copy.50
  379.3 18.6 %all_to_all.114 = bf16[64,8,1024]{2,1,0:T(8,128)(2,1)S(1)} all-to-all(bf16[64,8,1024]{2,1,0:T(8,128)(2,1)S(1)} %copy.50), channel_id=1, replica_groups=mesh['ctx'=16,'tp'=8] {'ctx'}, dimensions={0} | all-to-all | bytes 2097152 | tf_op jit(solution)/shard_map/all_to_all | solution.py:111
  397.8 0.2 copy.51
  398.1 0.0 copy-done.2
  398.1 0.0 copy-done.3
  398.1 0.6 fusion.28
  398.7 15.6 %fusion.135 = f32[512,8192]{1,0:T(8,128)} fusion(bf16[512,1024]{1,0:T(8,128)(2,1)S(1)} %fusion.28, bf16[1024,8192]{1,0:T(8,128)(2,1)} %param.11), kind=kOutput, calls=%fused_computation.154 | convolution fusion | flops 8589934592 | bytes 34603008 | tf_op jit(solution)/shard_map/dot_general | solution.py:118
  414.3 0.0 reduce-scatter.2.cloned.1.call-update
  414.4 89.6 %reduce-scatter.2.cloned.1.call-done = f32[512,1024]{1,0:T(8,128)} async-done(((f32[512,8192]{1,0:T(8,128)}), f32[512,1024]{1,0:T(8,128)}) %reduce-scatter.2.cloned.1.call-update) | async-done | bytes 2097168 | tf_op jit(solution)/shard_map/reduce_scatter | solution.py:119
  504.0 2.7 convert_element_type.137
  (1 shorter events, 0.0 us)
Async XLA Ops:
  10.3 25.8 %all-to-all-start = ((bf16[4,128,1024]{2,0,1:T(4,128)(2,1)}), bf16[4,128,1024]{2,0,1:T(4,128)(2,1)S(1)}, u32[]{:S(2)}, u32[]{:S(2)}) async-start(bf16[4,128,1024]{2,0,1:T(4,128)(2,1)} %copy.35), calls=%async_computation | async-start | bytes 2097152 | tf_op jit(solution)/shard_map/all_to_all | solution.py:88
  36.1 57.3 %all-to-all-start.3 = ((bf16[2,8,128,1024]{3,1,0,2:T(8,128)(2,1)}), bf16[2,8,128,1024]{3,1,0,2:T(8,128)(2,1)}, u32[]{:S(2)}, u32[]{:S(2)}) async-start(bf16[2,8,128,1024]{3,1,0,2:T(8,128)(2,1)} %copy.42), calls=%async_computation.3 | async-start | bytes 8388608 | tf_op jit(solution)/shard_map/all_to_all | solution.py:90
  93.4 54.6 %all-to-all-start.1 = ((f32[128,8,1024]{2,1,0:T(8,128)}), f32[128,8,1024]{2,1,0:T(8,128)}, u32[]{:S(2)}, u32[]{:S(2)}) async-start(f32[128,8,1024]{2,1,0:T(8,128)} %copy.38), calls=%async_computation.1 | async-start | bytes 8388608 | tf_op jit(solution)/shard_map/all_to_all | solution.py:95
  148.0 58.3 %all-to-all-start.2 = ((f32[128,8,1024]{2,1,0:T(8,128)}), f32[128,8,1024]{2,1,0:T(8,128)}, u32[]{:S(2)}, u32[]{:S(2)}) async-start(f32[128,8,1024]{2,1,0:T(8,128)} %copy.40), calls=%async_computation.2 | async-start | bytes 8388608 | tf_op jit(solution)/shard_map/all_to_all | solution.py:96
  206.3 16.7 %copy-start = (f32[1,16,8,8,1024]{4,3,1,2,0:T(8,128)S(1)}, f32[1,16,8,8,1024]{4,3,1,2,0:T(8,128)}, u32[]{:S(2)}) copy-start(f32[1,16,8,8,1024]{4,3,1,2,0:T(8,128)} %get-tuple-element.11) | copy-start | bytes 12582916
  206.3 16.7 %copy-start.1 = (f32[1,16,8,8,1024]{4,3,1,2,0:T(8,128)S(1)}, f32[1,16,8,8,1024]{4,3,1,2,0:T(8,128)}, u32[]{:S(2)}) copy-start(f32[1,16,8,8,1024]{4,3,1,2,0:T(8,128)} %get-tuple-element.12) | copy-start | bytes 12582916
  259.9 56.1 %all-to-all-start.5 = ((f32[128,8,1024]{2,1,0:T(8,128)}), f32[128,8,1024]{2,1,0:T(8,128)}, u32[]{:S(2)}, u32[]{:S(2)}) async-start(f32[128,8,1024]{2,1,0:T(8,128)} %copy.48), calls=%async_computation.5 | async-start | bytes 8388608 | tf_op jit(solution)/shard_map/all_to_all | solution.py:108
  316.0 57.3 %all-to-all-start.4 = ((f32[128,8,1024]{2,1,0:T(8,128)}), f32[128,8,1024]{2,1,0:T(8,128)}, u32[]{:S(2)}, u32[]{:S(2)}) async-start(f32[128,8,1024]{2,1,0:T(8,128)} %copy.46), calls=%async_computation.4 | async-start | bytes 8388608 | tf_op jit(solution)/shard_map/all_to_all | solution.py:107
  321.7 182.3 %reduce-scatter.2.cloned.1.call-start = ((), (), s32[]{:S(2)}) async-start(), calls=%async_computation.8 | async-start | bytes 18874368 | tf_op jit(solution)/shard_map/reduce_scatter | solution.py:119
  378.6 19.4 %copy-start.2 = (bf16[512,1024]{1,0:T(8,128)(2,1)S(1)}, bf16[512,1024]{1,0:T(8,128)(2,1)}, u32[]{:S(2)}) copy-start(bf16[512,1024]{1,0:T(8,128)(2,1)} %param.6) | copy-start | bytes 3145732
  378.7 19.4 %copy-start.3 = (f32[1024]{0:T(1024)S(1)}, f32[1024]{0:T(1024)}, u32[]{:S(2)}) copy-start(f32[1024]{0:T(1024)} %param.10) | copy-start | bytes 12292
Sparse Core Ops, SparseCore 0:
  414.5 89.4 reduce-scatter.1
where the time goes:
time: 524 us; the launch traced here: 514 us
  waiting for transfers between devices  299 us (57%)
  matrix products  94.6 us (18%)
  local copies, waits for them, and re-layouts  39 us (7%)
  starting transfers between devices  35.7 us (7%)
  blocking collectives  18.6 us (4%)
  between operations  13.8 us (3%)
  other arithmetic  12.7 us (2%)
    reduce_scatter x1, waiting for transfers between devices, per_device(): lax.psum_scatter(terms, 'tp', scatter_dimension=1, tiled=True)  89.6 us
    all_to_all x1, waiting for transfers between devices, per_device(): lax.all_to_all(real_c, 'ctx', split_axis=0, concat_axis=1, tiled=True)  45.5 us
    all_to_all x1, waiting for transfers between devices, per_device(): lax.all_to_all(imag_c, 'ctx', split_axis=0, concat_axis=1, tiled=True)  44.2 us
    all_to_all x1, waiting for transfers between devices, per_device(): lax.all_to_all(real_a, 'ctx', split_axis=0, concat_axis=1, tiled=True)  43.1 us
    all_to_all x1, waiting for transfers between devices, per_device(): lax.all_to_all(spec_parts, 'ctx', split_axis=2, concat_axis=1, tiled=True)  39.4 us
    all_to_all x1, waiting for transfers between devices, per_device(): lax.all_to_all(imag_a, 'ctx', split_axis=0, concat_axis=1, tiled=True)  26.3 us
    all_to_all x1, blocking collectives, per_device(): lax.all_to_all(filtered_cols, 'ctx', split_axis=0, concat_axis=1, tiled=T...  18.6 us
    dot_general x1, matrix products, middle(): jnp.einsum('kn,mnc->kmc', cos_cols, imag_in, precision=highest)  16.7 us
  transfers between devices with their start and end apart: 7, of which 7 were waited for; matrix products, arithmetic and copies ran while one was open for 12% of the time, Pallas kernels for 0%

commit v1 on v0

v1 whole, which is shorter than its diff:
```python
import functools
import math

import numpy as np

import jax
import jax.numpy as jnp
from jax import lax
from jax.experimental import pallas as pl
from jax.experimental.pallas import tpu as pltpu
from jax.sharding import PartitionSpec as P

ROWS = 256
HALF = 17
F32 = jnp.float32
BF16 = jnp.bfloat16
BIG = 56 * 1024 * 1024


def tables():
    a = np.arange(16)
    e = np.arange(HALF)
    angle = 2.0 * np.pi * np.outer(e, a) / 32.0
    first = np.concatenate([np.cos(angle), -np.sin(angle[1:16])], axis=0)
    last = np.concatenate([np.cos(angle), -np.sin(angle[1:16])], axis=0).T
    eye = np.eye(16)
    first = np.kron(first, eye)
    last = np.kron(last, eye) / 16384.0
    r = np.arange(ROWS)
    angle = 2.0 * np.pi * (np.outer(r, r) % ROWS) / ROWS
    c, s = np.cos(angle), np.sin(angle)
    forward = np.block([[c, s], [-s, c]])
    backward = np.block([[c, -s], [s, c]])
    lane = np.arange(128) // 64
    place = 256 * lane[None, :] + r[:, None]
    angle = 2.0 * np.pi * ((e[:, None, None] * place[None]) % 16384) / 16384.0
    turn = np.stack([np.cos(angle), -np.sin(angle)], axis=1)
    angle = 2.0 * np.pi * (lane[None, :] * r[:, None]) / 512.0
    side = np.stack([np.cos(angle), -np.sin(angle)])
    return first, last, forward, backward, turn, side


def shuffles():
    index = np.arange(16)
    plain = np.zeros((256, 256))
    turned = np.zeros((256, 256))
    for e in range(16):
        plain[16 * e + index, 16 * index + e] = 1.0
        turned[16 * e + 15 - index, 16 * index + e] = 1.0
    return np.stack([plain, turned])


def low_lanes(shape):
    return lax.broadcasted_iota(jnp.int32, shape, len(shape) - 1) < 64


def interleave(top, bottom):
    low = low_lanes(top.shape)
    even = jnp.where(low, top, pltpu.roll(bottom, 64, 1))
    odd = jnp.where(low, pltpu.roll(top, 64, 1), bottom)
    return even, odd


def pack_signal_kernel(key_ref, value_ref, out_ref):
    for b in range(8):
        lanes = slice(128 * b, 128 * b + 128)
        s = key_ref[:, lanes].astype(F32) * value_ref[:, lanes].astype(F32)
        even, odd = interleave(s[:ROWS], s[ROWS:])
        out_ref[2 * b] = even.astype(BF16)
        out_ref[2 * b + 1] = odd.astype(BF16)


def pack_signal(key_proj, value_proj):
    return pl.pallas_call(
        pack_signal_kernel,
        out_shape=jax.ShapeDtypeStruct((16, ROWS, 128), BF16),
        compiler_params=pltpu.CompilerParams(vmem_limit_bytes=BIG),
        name="pack_signal",
    )(key_proj, value_proj)


def pack_spectrum_kernel(shuffle_ref, spec_ref, out_ref):
    width = spec_ref.shape[2]
    rows = spec_ref[0].reshape(16, 2, 2, 16, width)
    for high in range(2):
        parts = []
        for g in range(2):
            part = rows[:, g, high].reshape(256, width)
            parts.append(jnp.dot(shuffle_ref[high], part, preferred_element_type=F32))
        if high:
            parts = parts[::-1]
        for b in range(width // 128):
            lanes = slice(128 * b, 128 * b + 128)
            even, odd = interleave(parts[0][:, lanes], parts[1][:, lanes])
            keep = slice(16 * high, 16 * high + 16)
            out_ref[2 * b, 0, keep] = even.astype(BF16).reshape(16, 16, 128)
            out_ref[2 * b + 1, 0, keep] = odd.astype(BF16).reshape(16, 16, 128)


def pack_spectrum(filter_spectrum, shuffle):
    width = 256
    return pl.pallas_call(
        pack_spectrum_kernel,
        grid=(2, 1024 // width),
        in_specs=[
            pl.BlockSpec((2, 256, 256), lambda i, j: (0, 0, 0)),
            pl.BlockSpec((1, 1024, width), lambda i, j: (i, 0, j)),
        ],
        out_specs=pl.BlockSpec((width // 64, 1, 32, 16, 128), lambda i, j: (j, i, 0, 0, 0)),
        out_shape=jax.ShapeDtypeStruct((16, 2, 32, 16, 128), BF16),
        compiler_params=pltpu.CompilerParams(vmem_limit_bytes=BIG),
        name="pack_spectrum",
    )(shuffle, filter_spectrum)


def sign_lanes(shape):
    return jnp.where(low_lanes(shape), 1.0, -1.0).astype(F32)


def forward_kernel(first_ref, turn_ref, side_ref, signal_ref, out_ref):
    sign = sign_lanes((16, 128))

    def step(q, carry):
        at = pl.ds(pl.multiple_of(16 * q, 16), 16)
        block = signal_ref[:, at, :].reshape(256, 128)
        sums = jnp.dot(first_ref[...], block, preferred_element_type=F32).reshape(32, 16, 128)
        side_re = side_ref[0, at, :]
        side_im = side_ref[1, at, :]
        for e in range(HALF):
            re = sums[e]
            cos = turn_ref[e, 0, at, :]
            sin = turn_ref[e, 1, at, :]
            if e in (0, 16):
                c_re, c_im = re * cos, re * sin
            else:
                im = sums[16 + e]
                c_re, c_im = re * cos - im * sin, re * sin + im * cos
            d_re = c_re * sign + pltpu.roll(c_re, 64, 1)
            d_im = c_im * sign + pltpu.roll(c_im, 64, 1)
            out_ref[e, 0, at, :] = (d_re * side_re - d_im * side_im).astype(BF16)
            out_ref[e, 1, at, :] = (d_re * side_im + d_im * side_re).astype(BF16)
        return carry

    lax.fori_loop(0, 16, step, 0)


def forward_part(signal, first, turn, side):
    return pl.pallas_call(
        forward_kernel,
        out_shape=jax.ShapeDtypeStruct((HALF, 2, ROWS, 128), BF16),
        compiler_params=pltpu.CompilerParams(vmem_limit_bytes=BIG),
        name="forward_part",
    )(first, turn, side, signal)


def filter_kernel(
    forward_ref, backward_ref, last_ref, turn_ref, side_ref, part_ref, spec_ref, out_ref, held
):
    sign = sign_lanes((ROWS, 128))
    side_re = side_ref[0]
    side_im = side_ref[1]

    def spectrum(which, e):
        return spec_ref[:, which, e].astype(F32).reshape(ROWS, 128)

    def mirrored(which, e):
        return jnp.concatenate([spec_ref[15 - j, which, e] for j in range(16)], axis=0).astype(F32)

    for start in range(0, HALF, 2):
        group = [e for e in (start, start + 1) if e < HALF]
        data = jnp.concatenate([part_ref[e].reshape(512, 128) for e in group], axis=1)
        x = jnp.dot(forward_ref[...], data, preferred_element_type=F32)
        products = []
        for n, e in enumerate(group):
            x_re = x[:ROWS, 128 * n : 128 * n + 128]
            x_im = x[ROWS:, 128 * n : 128 * n + 128]
            if e == 0:
                h_re, h_im = spectrum(0, 0), spectrum(1, 0)
            elif e == 16:
                h_re, h_im = mirrored(0, 16), -mirrored(1, 16)
            else:
                h_re = spectrum(0, e) + mirrored(0, 32 - e)
                h_im = spectrum(1, e) - mirrored(1, 32 - e)
            y_re = x_re * h_re - x_im * h_im
            y_im = x_re * h_im + x_im * h_re
            products.append(jnp.concatenate([y_re.astype(BF16), y_im.astype(BF16)], axis=0))
        back = jnp.dot(
            backward_ref[...], jnp.concatenate(products, axis=1), preferred_element_type=F32
        )
        for n, e in enumerate(group):
            b_re = back[:ROWS, 128 * n : 128 * n + 128]
            b_im = back[ROWS:, 128 * n : 128 * n + 128]
            s_re = b_re * side_re + b_im * side_im
            s_im = b_im * side_re - b_re * side_im
            c_re = s_re * sign + pltpu.roll(s_re, 64, 1)
            c_im = s_im * sign + pltpu.roll(s_im, 64, 1)
            cos = turn_ref[e, 0]
            sin = turn_ref[e, 1]
            held[e] = (c_re * cos + c_im * sin).astype(BF16)
            if e not in (0, 16):
                held[16 + e] = (c_im * cos - c_re * sin).astype(BF16)

    def step(q, carry):
        at = pl.ds(pl.multiple_of(16 * q, 16), 16)
        block = held[:, at, :].reshape(512, 128)
        y = jnp.dot(last_ref[...], block, preferred_element_type=F32)
        out_ref[:, at, :] = y.astype(BF16).reshape(16, 16, 128)
        return carry

    lax.fori_loop(0, 16, step, 0)


def filter_part(part, spectrum, forward, backward, last, turn, side):
    return pl.pallas_call(
        filter_kernel,
        out_shape=jax.ShapeDtypeStruct((16, ROWS, 128), BF16),
        scratch_shapes=[pltpu.VMEM((32, ROWS, 128), BF16)],
        compiler_params=pltpu.CompilerParams(vmem_limit_bytes=BIG),
        name="filter_part",
    )(forward, backward, last, turn, side, part, spectrum)


def project_kernel(query_ref, key_ref, value_ref, skip_ref, filtered_ref, weight_ref, out_ref, gated):
    @pl.when(pl.program_id(0) == 0)
    def _():
        for b in range(8):
            lanes = slice(128 * b, 128 * b + 128)
            top, bottom = interleave(
                filtered_ref[2 * b].astype(F32), filtered_ref[2 * b + 1].astype(F32)
            )
            for n, filtered in enumerate((top, bottom)):
                rows = slice(ROWS * n, ROWS * n + ROWS)
                signal = key_ref[rows, lanes].astype(F32) * value_ref[rows, lanes].astype(F32)
                signal = signal.astype(BF16).astype(F32)
                gate = filtered + skip_ref[:, lanes] * signal
                gated[rows, lanes] = (query_ref[rows, lanes].astype(F32) * gate).astype(BF16)

    out_ref[0] = jnp.dot(gated[...], weight_ref[...], preferred_element_type=F32).astype(BF16)


def project(query_proj, key_proj, value_proj, skip_gain, filtered, out_weight):
    rows, channels = query_proj.shape
    width = 1024
    blocks = out_weight.shape[1] // width
    whole = lambda i: (0, 0)
    return pl.pallas_call(
        project_kernel,
        grid=(blocks,),
        in_specs=[
            pl.BlockSpec((rows, channels), whole),
            pl.BlockSpec((rows, channels), whole),
            pl.BlockSpec((rows, channels), whole),
            pl.BlockSpec((1, channels), whole),
            pl.BlockSpec((16, ROWS, 128), lambda i: (0, 0, 0)),
            pl.BlockSpec((channels, width), lambda i: (0, i)),
        ],
        out_specs=pl.BlockSpec((1, rows, width), lambda i: (i, 0, 0)),
        out_shape=jax.ShapeDtypeStruct((blocks, rows, width), BF16),
        scratch_shapes=[pltpu.VMEM((rows, channels), BF16)],
        compiler_params=pltpu.CompilerParams(vmem_limit_bytes=BIG),
        name="project",
    )(query_proj, key_proj, value_proj, skip_gain.reshape(1, channels), filtered, out_weight)


def convolve(key_proj, value_proj, filter_spectrum):
    first, last, forward, backward, turn, side = tables()
    as_bf16 = lambda t: jnp.asarray(t.astype(np.float32)).astype(BF16)
    turn = jnp.asarray(turn.astype(np.float32))
    side = jnp.asarray(side.astype(np.float32))
    signal = pack_signal(key_proj, value_proj)
    signal = lax.all_to_all(signal, "ctx", split_axis=0, concat_axis=0, tiled=True)
    spectrum = pack_spectrum(filter_spectrum, as_bf16(shuffles()))
    spectrum = lax.all_to_all(spectrum, "ctx", split_axis=0, concat_axis=0, tiled=True)
    part = forward_part(signal, as_bf16(first), turn, side)
    out = filter_part(
        part, spectrum, as_bf16(forward), as_bf16(backward), as_bf16(last), turn, side
    )
    return lax.all_to_all(out, "ctx", split_axis=0, concat_axis=0, tiled=True)


def per_device(query_proj, key_proj, value_proj, filter_spectrum, skip_gain, out_weight):
    filtered = convolve(key_proj, value_proj, filter_spectrum)
    terms = project(query_proj, key_proj, value_proj, skip_gain, filtered, out_weight)
    out = lax.psum_scatter(terms, "tp", scatter_dimension=0, tiled=True)
    return out[0]


def solution(mesh):
    in_specs = (
        P("ctx", "tp"),
        P("ctx", "tp"),
        P("ctx", "tp"),
        P(None, "ctx", "tp"),
        P("tp"),
        P("tp", None),
    )
    out_specs = P("ctx", "tp")
    return jax.shard_map(
        per_device, mesh=mesh, in_specs=in_specs, out_specs=out_specs, check_vma=False
    )
```

time: 524 us -> 200 us (0.38); the launches traced: 514 us -> 199 us
  waiting for transfers between devices: 299 us -> 104 us
  matrix products: 94.6 us -> 0 us
  Pallas kernels: 0 us -> 50.1 us
  local copies, waits for them, and re-layouts: 39 us -> 0.97 us
  starting transfers between devices: 35.7 us -> 12.7 us
  other arithmetic: 12.7 us -> 0 us
    all_to_all x6 -> x2, waiting for transfers between devices: 210 us -> 53.4 us  [the longest x1 43.6 us: convolve(): lax.all_to_all(spectrum, 'ctx', split_axis=0, concat_axis=0, tiled=True)]
    dot_general x12 -> x0, matrix products: 94.6 us -> none  [the longest x1 16.7 us: middle(): jnp.einsum('kn,mnc->kmc', cos_cols, imag_in, precision=highest)]
    pallas_call x0 -> x5, Pallas kernels: none -> 50.1 us  [the longest x1 17.5 us: project(): pl.pallas_call(project_kernel, grid=(blocks,), in_specs=[pl.BlockSpec((ro...]
    reduce_scatter x1, waiting for transfers between devices: 89.6 us -> 50.3 us  [per_device(): out = lax.psum_scatter(terms, 'tp', scatter_dimension=0, tiled=True)]
    all_to_all x6 -> x2, starting transfers between devices: 35.5 us -> 12.7 us  [the longest x1 8.13 us: convolve(): lax.all_to_all(signal, 'ctx', split_axis=0, concat_axis=0, tiled=True)]
    sub x2 -> x0, local copies, waits for them, and re-layouts: 13.2 us -> none  [the longest x1 6.62 us: middle(): return (ur * tw_cos - ui * tw_sin, ui * tw_cos + ur * tw_sin)]
    convert_element_type x6 -> x0, other arithmetic: 9.8 us -> none  [the longest x1 4.24 us: per_device(): spec_rows[0].astype(jnp.float32)]
    add x2 -> x0, local copies, waits for them, and re-layouts: 8.74 us -> none  [the longest x1 4.38 us: middle(): return (ur * tw_cos - ui * tw_sin, ui * tw_cos + ur * tw_sin)]
  transfers between devices with their start and end apart: 7 -> 3, of which waited for: 7 -> 3; matrix products, arithmetic and copies ran while one was open for 12% -> 0% of each run, Pallas kernels for 0% -> 9%
where the time goes in v1:
time: 200 us; the launch traced here: 199 us
  waiting for transfers between devices  104 us (52%)
  Pallas kernels  50.1 us (25%)
  blocking collectives  18.1 us (9%)
  between operations  13.4 us (7%)
  starting transfers between devices  12.7 us (6%)
    reduce_scatter x1, waiting for transfers between devices, per_device(): out = lax.psum_scatter(terms, 'tp', scatter_dimension=0, tiled=True)  50.3 us
    all_to_all x1, waiting for transfers between devices, convolve(): lax.all_to_all(spectrum, 'ctx', split_axis=0, concat_axis=0, tiled=True)  43.6 us
    all_to_all x1, blocking collectives, convolve(): return lax.all_to_all(out, 'ctx', split_axis=0, concat_axis=0, tiled=True)  18.1 us
    pallas_call x1, Pallas kernels, project(): pl.pallas_call(project_kernel, grid=(blocks,), in_specs=[pl.BlockSpec((ro...  17.5 us
    pallas_call x1, Pallas kernels, filter_part(): pl.pallas_call(filter_kernel, out_shape=jax.ShapeDtypeStruct((16, ROWS, 1...  12.6 us
    all_to_all x1, waiting for transfers between devices, convolve(): lax.all_to_all(signal, 'ctx', split_axis=0, concat_axis=0, tiled=True)  9.78 us
    pallas_call x1, Pallas kernels, forward_part(): pl.pallas_call(forward_kernel, out_shape=jax.ShapeDtypeStruct((HALF, 2, R...  9.12 us
    all_to_all x1, starting transfers between devices, convolve(): lax.all_to_all(signal, 'ctx', split_axis=0, concat_axis=0, tiled=True)  8.13 us
  transfers between devices with their start and end apart: 3, of which 3 were waited for; matrix products, arithmetic and copies ran while one was open for 0% of the time, Pallas kernels for 9%

profile of v1, /device:TPU:0, one launch (start us, length us, event | category | flops | bytes accessed | tf_op | source)
XLA Modules:
  0.0 199.1 jit_solution(1605203296841458285)
XLA Ops:
  6.5 3.1 %pack_signal.1 = bf16[16,256,128]{2,1,0:T(8,128)(2,1)} custom-call(bf16[512,1024]{1,0:T(8,128)(2,1)} %key_ref.3, bf16[512,1024]{1,0:T(8,128)(2,1)} %value_ref.3), custom_call_target="tpu_custom_call" | custom-call | tf_op jit(solution)/shard_map/pack_signal/pallas_call | solution.py:74
  9.6 8.1 %all-to-all-start = ((bf16[16,256,128]{2,1,0:T(8,128)(2,1)}), bf16[16,256,128]{2,1,0:T(8,128)(2,1)S(1)}, u32[]{:S(2)}, u32[]{:S(2)}) async-start(bf16[16,256,128]{2,1,0:T(8,128)(2,1)} %pack_signal.1), calls=%async_computation | async-start | bytes 2097152 | tf_op jit(solution)/shard_map/all_to_all | solution.py:271
  17.7 7.9 %pack_spectrum.1 = bf16[16,2,32,16,128]{4,3,2,1,0:T(8,128)(2,1)} custom-call(bf16[2,256,256]{2,1,0:T(8,128)(2,1)} %constant.25.shuffle_ref, bf16[2,1024,1024]{2,1,0:T(8,128)(2,1)} %spec_ref.1), custom_call_target="tpu_custom_call" | custom-call | tf_op jit(solution)/shard_map/pack_spectrum/pallas_call | solution.py:102
  25.6 9.8 %all-to-all-done.signal_ref = bf16[16,256,128]{2,1,0:T(8,128)(2,1)S(1)} async-done(((bf16[16,256,128]{2,1,0:T(8,128)(2,1)}), bf16[16,256,128]{2,1,0:T(8,128)(2,1)S(1)}, u32[]{:S(2)}, u32[]{:S(2)}) %all-to-all-start) | async-done | bytes 1048608 | tf_op jit(solution)/shard_map/all_to_all | solution.py:271
  35.4 0.0 copy-start
  35.4 1.0 copy-done
  36.4 4.5 %all-to-all-start.1 = ((bf16[16,2,32,16,128]{4,3,2,1,0:T(8,128)(2,1)}), bf16[16,2,32,16,128]{4,3,2,1,0:T(8,128)(2,1)}, u32[]{:S(2)}, u32[]{:S(2)}) async-start(bf16[16,2,32,16,128]{4,3,2,1,0:T(8,128)(2,1)} %pack_spectrum.1), calls=%async_computation.1 | async-start | bytes 8388608 | tf_op jit(solution)/shard_map/all_to_all | solution.py:273
  40.9 0.0 reduce-scatter.2.cloned.1.call-start
  41.0 9.1 %forward_part.1.part_ref = bf16[17,2,256,128]{3,2,1,0:T(8,128)(2,1)} custom-call(bf16[512,256]{1,0:T(8,128)(2,1)} %constant.24.first_ref, f32[17,2,256,128]{3,2,1,0:T(8,128)} %constant.14.clone.turn_ref, f32[2,256,128]{2,1,0:T(8,128)} %constant.15.clone.side_ref, bf16[16,256,128]{2,1,0:T(8,128)(2,1)} %copy-done), custom_call_target="tpu_custom_call" | custom-call | tf_op jit(solution)/shard_map/forward_part/pallas_call | solution.py:148
  50.1 43.6 %all-to-all-done.1.spec_ref = bf16[16,2,32,16,128]{4,3,2,1,0:T(8,128)(2,1)} async-done(((bf16[16,2,32,16,128]{4,3,2,1,0:T(8,128)(2,1)}), bf16[16,2,32,16,128]{4,3,2,1,0:T(8,128)(2,1)}, u32[]{:S(2)}, u32[]{:S(2)}) %all-to-all-start.1) | async-done | bytes 4194336 | tf_op jit(solution)/shard_map/all_to_all | solution.py:273
  93.7 12.6 %filter_part.1 = bf16[16,256,128]{2,1,0:T(8,128)(2,1)} custom-call(bf16[512,512]{1,0:T(8,128)(2,1)} %constant.21.forward_ref, bf16[512,512]{1,0:T(8,128)(2,1)} %constant.22.backward_ref, bf16[256,512]{1,0:T(8,128)(2,1)} %constant.23.last_ref, f32[17,2,256,128]{3,2,1,0:T(8,128)} %constant.14.clone.turn_ref, f32[2,256,128]{2,1,0:T(8,128)} %constant.15.clone.side_ref, ...), custom_call_target="tpu_custom_call" | custom-call | tf_op jit(solution)/shard_map/filter_part/pallas_call | solution.py:214
  106.3 18.1 %all_to_all.15.filtered_ref = bf16[16,256,128]{2,1,0:T(8,128)(2,1)} all-to-all(bf16[16,256,128]{2,1,0:T(8,128)(2,1)} %filter_part.1), channel_id=1, replica_groups=mesh['ctx'=16,'tp'=8] {'ctx'}, dimensions={0} | all-to-all | bytes 2097152 | tf_op jit(solution)/shard_map/all_to_all | solution.py:278
  124.4 17.5 %project.1 = bf16[8,512,1024]{2,1,0:T(8,128)(2,1)} custom-call(bf16[512,1024]{1,0:T(8,128)(2,1)} %query_ref.1, bf16[512,1024]{1,0:T(8,128)(2,1)} %key_ref.3, bf16[512,1024]{1,0:T(8,128)(2,1)} %value_ref.3, f32[1,1024]{1,0:T(1,128)} %bitcast.2, bf16[16,256,128]{2,1,0:T(8,128)(2,1)} %all_to_all.15.filtered_ref, bf16[1024,8192]{1,0:T(8,128)(2,1)} %weight_ref.1), custom_call_target="tpu_custom_call" | custom-call | tf_op jit(solution)/shard_map/project/pallas_call | solution.py:246
  141.9 0.0 reduce-scatter.2.cloned.1.call-update
  141.9 50.3 %reduce-scatter.2.cloned.1.call-done = bf16[1,512,1024]{2,1,0:T(8,128)(2,1)} async-done(((bf16[8,512,1024]{2,1,0:T(8,128)(2,1)}), bf16[1,512,1024]{2,1,0:T(8,128)(2,1)}) %reduce-scatter.2.cloned.1.call-update) | async-done | bytes 1048592 | tf_op jit(solution)/shard_map/reduce_scatter | solution.py:284
Async XLA Ops:
  9.6 25.8 %all-to-all-start = ((bf16[16,256,128]{2,1,0:T(8,128)(2,1)}), bf16[16,256,128]{2,1,0:T(8,128)(2,1)S(1)}, u32[]{:S(2)}, u32[]{:S(2)}) async-start(bf16[16,256,128]{2,1,0:T(8,128)(2,1)} %pack_signal.1), calls=%async_computation | async-start | bytes 2097152 | tf_op jit(solution)/shard_map/all_to_all | solution.py:271
  35.4 1.0 copy-start
  36.4 57.3 %all-to-all-start.1 = ((bf16[16,2,32,16,128]{4,3,2,1,0:T(8,128)(2,1)}), bf16[16,2,32,16,128]{4,3,2,1,0:T(8,128)(2,1)}, u32[]{:S(2)}, u32[]{:S(2)}) async-start(bf16[16,2,32,16,128]{4,3,2,1,0:T(8,128)(2,1)} %pack_spectrum.1), calls=%async_computation.1 | async-start | bytes 8388608 | tf_op jit(solution)/shard_map/all_to_all | solution.py:273
  40.9 151.3 %reduce-scatter.2.cloned.1.call-start = ((), (), s32[]{:S(2)}) async-start(), calls=%async_computation.4 | async-start | bytes 9437184 | tf_op jit(solution)/shard_map/reduce_scatter | solution.py:284
Sparse Core Ops, SparseCore 0:
  142.0 50.1 reduce-scatter.1

commit v2 on v1

v2 whole, which is shorter than its diff:
```python
import functools

import numpy as np

import jax
import jax.numpy as jnp
from jax import lax
from jax.experimental import pallas as pl
from jax.experimental.pallas import tpu as pltpu
from jax.sharding import PartitionSpec as P

ROWS = 256
HALF = 17
HELD = pl.BlockSpec(memory_space=pltpu.VMEM)
FAR = pl.BlockSpec(memory_space=pltpu.HBM)
SCALARS = pl.BlockSpec(memory_space=pltpu.SMEM)
F32 = jnp.float32
BF16 = jnp.bfloat16
TIGHT = 56 * 1024 * 1024
BIG = 60 * 1024 * 1024
LITTLE = 24 * 1024 * 1024
MOST = 48 * 1024 * 1024


def tables():
    a = np.arange(16)
    e = np.arange(HALF)
    angle = 2.0 * np.pi * np.outer(e, a) / 32.0
    first = np.concatenate([np.cos(angle), -np.sin(angle[1:16])], axis=0)
    last = np.concatenate([np.cos(angle), -np.sin(angle[1:16])], axis=0).T
    eye = np.eye(16)
    first = np.kron(first, eye)
    last = np.kron(last, eye) / 16384.0
    r = np.arange(ROWS)
    angle = 2.0 * np.pi * (np.outer(r, r) % ROWS) / ROWS
    c, s = np.cos(angle), np.sin(angle)
    forward = np.block([[c, s], [-s, c]])
    backward = np.block([[c, -s], [s, c]])
    lane = np.arange(128) // 64
    place = 256 * lane[None, :] + r[:, None]
    angle = 2.0 * np.pi * ((e[:, None, None] * place[None]) % 16384) / 16384.0
    turn = np.stack([np.cos(angle), -np.sin(angle)], axis=1)
    angle = 2.0 * np.pi * (lane[None, :] * r[:, None]) / 512.0
    side = np.stack([np.cos(angle), -np.sin(angle)])
    return first, last, forward, backward, turn, side


def shuffles():
    index = np.arange(16)
    plain = np.zeros((256, 256))
    turned = np.zeros((256, 256))
    for e in range(16):
        plain[16 * e + index, 16 * index + e] = 1.0
        turned[16 * e + 15 - index, 16 * index + e] = 1.0
    return np.stack([plain, turned])


def low_lanes(shape):
    return lax.broadcasted_iota(jnp.int32, shape, len(shape) - 1) < 64


def interleave(top, bottom):
    low = low_lanes(top.shape)
    even = jnp.where(low, top, pltpu.roll(bottom, 64, 1))
    odd = jnp.where(low, pltpu.roll(top, 64, 1), bottom)
    return even, odd


def pack_signal_kernel(key_ref, value_ref, out_ref, keys, values, done):
    width = 256
    copies = []
    for n in range(4):
        lanes = pl.ds(width * n, width)
        pair = [
            pltpu.make_async_copy(source.at[:, lanes], target.at[:, lanes], done.at[m, n])
            for m, (source, target) in enumerate(((key_ref, keys), (value_ref, values)))
        ]
        for copy in pair:
            copy.start()
        copies.append(pair)
    for b in range(8):
        if b % 2 == 0:
            for copy in copies[b // 2]:
                copy.wait()
        lanes = slice(128 * b, 128 * b + 128)
        for r in range(0, ROWS, 32):
            halves = []
            for n in range(2):
                rows = slice(ROWS * n + r, ROWS * n + r + 32)
                halves.append(keys[rows, lanes].astype(F32) * values[rows, lanes].astype(F32))
            even, odd = interleave(*halves)
            out_ref[2 * b, r : r + 32] = even.astype(BF16)
            out_ref[2 * b + 1, r : r + 32] = odd.astype(BF16)


def pack_signal(key_proj, value_proj):
    return pl.pallas_call(
        pack_signal_kernel,
        in_specs=[FAR] * 2,
        out_shape=jax.ShapeDtypeStruct((16, ROWS, 128), BF16),
        scratch_shapes=[
            pltpu.VMEM(key_proj.shape, BF16),
            pltpu.VMEM(key_proj.shape, BF16),
            pltpu.SemaphoreType.DMA((2, 4)),
        ],
        compiler_params=pltpu.CompilerParams(vmem_limit_bytes=BIG),
        cost_estimate=pl.CostEstimate(flops=1 << 20, bytes_accessed=3 << 20, transcendentals=0),
        name="pack_signal",
    )(key_proj, value_proj)


def slot(e):
    if e == 16:
        return 1
    return 2 * e if e < 16 else 2 * (32 - e) + 1


def pack_spectrum_kernel(shuffle_ref, spec_ref, out_ref):
    width = 256
    for which in range(2):
        for start in range(0, spec_ref.shape[2], width):
            rows = spec_ref[which, :, start : start + width].reshape(16, 2, 2, 16, width)
            for high in range(2):
                parts = []
                for g in range(2):
                    part = rows[:, g, high].reshape(256, width)
                    parts.append(jnp.dot(shuffle_ref[high], part, preferred_element_type=F32))
                if high:
                    parts = parts[::-1]
                for b in range(width // 128):
                    lanes = slice(128 * b, 128 * b + 128)
                    even, odd = interleave(parts[0][:, lanes], parts[1][:, lanes])
                    to = start // 64 + 2 * b
                    for e in range(16):
                        keep = slice(16 * e, 16 * e + 16)
                        out_ref[to, which, slot(16 * high + e)] = even[keep].astype(BF16)
                        out_ref[to + 1, which, slot(16 * high + e)] = odd[keep].astype(BF16)


def pack_spectrum(filter_spectrum, shuffle):
    return pl.pallas_call(
        pack_spectrum_kernel,
        in_specs=[HELD] * 2,
        out_specs=HELD,
        out_shape=jax.ShapeDtypeStruct((16, 2, 32, 16, 128), BF16),
        compiler_params=pltpu.CompilerParams(vmem_limit_bytes=LITTLE),
        cost_estimate=pl.CostEstimate(flops=1 << 30, bytes_accessed=12 << 20, transcendentals=0),
        name="pack_spectrum",
    )(shuffle, filter_spectrum)


def sign_lanes(shape):
    return jnp.where(low_lanes(shape), 1.0, -1.0).astype(F32)


def forward_kernel(first_ref, forward_ref, turn_ref, side_ref, signal_ref, out_ref, part):
    sign = sign_lanes((16, 128))

    def step(q, carry):
        at = pl.ds(pl.multiple_of(16 * q, 16), 16)
        block = signal_ref[:, at, :].reshape(256, 128)
        sums = jnp.dot(first_ref[...], block, preferred_element_type=F32).reshape(32, 16, 128)
        side_re = side_ref[0, at, :]
        side_im = side_ref[1, at, :]
        for e in range(HALF):
            re = sums[e]
            cos = turn_ref[e, 0, at, :]
            sin = turn_ref[e, 1, at, :]
            if e in (0, 16):
                c_re, c_im = re * cos, re * sin
            else:
                im = sums[16 + e]
                c_re, c_im = re * cos - im * sin, re * sin + im * cos
            d_re = c_re * sign + pltpu.roll(c_re, 64, 1)
            d_im = c_im * sign + pltpu.roll(c_im, 64, 1)
            part[e, 0, at, :] = (d_re * side_re - d_im * side_im).astype(BF16)
            part[e, 1, at, :] = (d_re * side_im + d_im * side_re).astype(BF16)
        return carry

    lax.fori_loop(0, 16, step, 0)

    def pair(n, carry):
        data = jnp.concatenate(
            [part[2 * n].reshape(512, 128), part[2 * n + 1].reshape(512, 128)], axis=1
        )
        x = jnp.dot(forward_ref[...], data, preferred_element_type=F32).astype(BF16)
        out_ref[2 * n] = x[:, :128].reshape(2, ROWS, 128)
        out_ref[2 * n + 1] = x[:, 128:].reshape(2, ROWS, 128)
        return carry

    lax.fori_loop(0, 8, pair, 0)
    x = jnp.dot(forward_ref[...], part[16].reshape(512, 128), preferred_element_type=F32)
    out_ref[16] = x.astype(BF16).reshape(2, ROWS, 128)


def forward_part(signal, first, forward, turn, side):
    return pl.pallas_call(
        forward_kernel,
        in_specs=[HELD] * 5,
        out_specs=HELD,
        out_shape=jax.ShapeDtypeStruct((HALF, 2, ROWS, 128), BF16),
        scratch_shapes=[pltpu.VMEM((HALF, 2, ROWS, 128), BF16)],
        compiler_params=pltpu.CompilerParams(vmem_limit_bytes=MOST),
        cost_estimate=pl.CostEstimate(flops=2 << 30, bytes_accessed=12 << 20, transcendentals=0),
        name="forward_part",
    )(first, forward, turn, side, signal)


def filter_kernel(
    backward_from,
    last_from,
    side_from,
    turn_from,
    x_ref,
    spec_ref,
    out_ref,
    backward_ref,
    last_ref,
    side_ref,
    turn_ref,
    held,
    products,
    sums,
    table_done,
    turn_done,
):
    tables = [
        pltpu.make_async_copy(source, target, table_done.at[n])
        for n, (source, target) in enumerate(
            ((backward_from, backward_ref), (side_from, side_ref), (last_from, last_ref))
        )
    ]
    turns = []
    for g in range(9):
        some = pl.ds(2 * g, 2 if g < 8 else 1)
        turns.append(
            pltpu.make_async_copy(turn_from.at[some], turn_ref.at[some], turn_done.at[g])
        )
    for copy in tables[:2] + turns + tables[2:]:
        copy.start()
    sign = sign_lanes((16, 128))

    def spectrum(j, which, place):
        return spec_ref[j, which, place].astype(F32)

    def filter_at(e, j):
        if e == 0:
            return spectrum(j, 0, 0), spectrum(j, 1, 0)
        if e == 16:
            return spectrum(15 - j, 0, 1), -spectrum(15 - j, 1, 1)
        h_re = spectrum(j, 0, 2 * e) + spectrum(15 - j, 0, 2 * e + 1)
        h_im = spectrum(j, 1, 2 * e) - spectrum(15 - j, 1, 2 * e + 1)
        return h_re, h_im

    for start in range(0, HALF, 2):
        group = range(start, min(start + 2, HALF))
        for n, e in enumerate(group):
            lanes = slice(128 * n, 128 * n + 128)
            for j in range(16):
                rows = slice(16 * j, 16 * j + 16)
                below = slice(ROWS + 16 * j, ROWS + 16 * j + 16)
                h_re, h_im = filter_at(e, j)
                x_re, x_im = x_ref[e, 0, rows].astype(F32), x_ref[e, 1, rows].astype(F32)
                products[start // 2, rows, lanes] = (x_re * h_re - x_im * h_im).astype(BF16)
                products[start // 2, below, lanes] = (x_re * h_im + x_im * h_re).astype(BF16)
        wide = 128 * len(group)
        if start == 0:
            tables[0].wait()
        sums[start // 2, :, :wide] = jnp.dot(
            backward_ref[...], products[start // 2, :, :wide], preferred_element_type=F32
        )
        if start == 0:
            tables[1].wait()
        turns[start // 2].wait()
        for n, e in enumerate(group):
            lanes = slice(128 * n, 128 * n + 128)
            for j in range(16):
                rows = slice(16 * j, 16 * j + 16)
                below = slice(ROWS + 16 * j, ROWS + 16 * j + 16)
                b_re = sums[start // 2, rows, lanes]
                b_im = sums[start // 2, below, lanes]
                side_re, side_im = side_ref[0, rows], side_ref[1, rows]
                s_re = b_re * side_re + b_im * side_im
                s_im = b_im * side_re - b_re * side_im
                c_re = s_re * sign + pltpu.roll(s_re, 64, 1)
                c_im = s_im * sign + pltpu.roll(s_im, 64, 1)
                cos, sin = turn_ref[e, 0, rows], turn_ref[e, 1, rows]
                held[e, rows] = (c_re * cos + c_im * sin).astype(BF16)
                if e not in (0, 16):
                    held[16 + e, rows] = (c_im * cos - c_re * sin).astype(BF16)

    tables[2].wait()
    for q in range(0, 16, 2):
        block = jnp.concatenate(
            [held[:, 16 * p : 16 * p + 16].reshape(512, 128) for p in (q, q + 1)], axis=1
        )
        y = jnp.dot(last_ref[...], block, preferred_element_type=F32).astype(BF16)
        for n in range(2):
            out_ref[:, 16 * (q + n) : 16 * (q + n) + 16] = y[:, 128 * n : 128 * n + 128].reshape(
                16, 16, 128
            )


def filter_part(x, spectrum, backward, last, turn, side):
    return pl.pallas_call(
        filter_kernel,
        in_specs=[FAR] * 4 + [HELD] * 2,
        out_specs=HELD,
        out_shape=jax.ShapeDtypeStruct((16, ROWS, 128), BF16),
        scratch_shapes=[
            *[pltpu.VMEM(t.shape, t.dtype) for t in (backward, last, side, turn)],
            pltpu.VMEM((32, ROWS, 128), BF16),
            pltpu.VMEM((9, 2 * ROWS, 256), BF16),
            pltpu.VMEM((9, 2 * ROWS, 256), F32),
            pltpu.SemaphoreType.DMA((3,)),
            pltpu.SemaphoreType.DMA((9,)),
        ],
        compiler_params=pltpu.CompilerParams(vmem_limit_bytes=TIGHT),
        cost_estimate=pl.CostEstimate(flops=2 << 30, bytes_accessed=16 << 20, transcendentals=0),
        name="filter_part",
    )(backward, last, side, turn, x, spectrum)


def gate_kernel(query_ref, key_ref, value_ref, skip_ref, filtered_ref, out_ref):
    for b in range(query_ref.shape[1] // 128):
        lanes = slice(128 * b, 128 * b + 128)
        skip = skip_ref[:, lanes]
        for r in range(0, ROWS, 32):
            halves = interleave(
                filtered_ref[2 * b, r : r + 32].astype(F32),
                filtered_ref[2 * b + 1, r : r + 32].astype(F32),
            )
            for n, filtered in enumerate(halves):
                rows = slice(ROWS * n + r, ROWS * n + r + 32)
                signal = key_ref[rows, lanes].astype(F32) * value_ref[rows, lanes].astype(F32)
                signal = signal.astype(BF16).astype(F32)
                held = filtered + skip * signal
                out_ref[rows, lanes] = (query_ref[rows, lanes].astype(F32) * held).astype(BF16)


def gate(query_proj, key_proj, value_proj, skip_gain, filtered):
    rows, channels = query_proj.shape
    return pl.pallas_call(
        gate_kernel,
        in_specs=[HELD] * 5,
        out_specs=HELD,
        out_shape=jax.ShapeDtypeStruct((rows, channels), BF16),
        compiler_params=pltpu.CompilerParams(vmem_limit_bytes=LITTLE),
        cost_estimate=pl.CostEstimate(flops=4 << 20, bytes_accessed=5 << 20, transcendentals=0),
        name="gate",
    )(query_proj, key_proj, value_proj, skip_gain.reshape(1, channels), filtered)


def far_kernel(own_ref, other_ref, weight_ref, other_weight_ref, top_ref, bottom_ref):
    width = 256
    for start in range(0, weight_ref.shape[1], width):
        lanes = slice(start, start + width)
        total = jnp.dot(own_ref[...], weight_ref[:, lanes], preferred_element_type=F32)
        total += jnp.dot(other_ref[...], other_weight_ref[:, lanes], preferred_element_type=F32)
        top_ref[:, lanes] = total[:ROWS].astype(BF16)
        bottom_ref[:, lanes] = total[ROWS:].astype(BF16)


def far_product(own, other, weight, other_weight):
    shape = jax.ShapeDtypeStruct((ROWS, weight.shape[1]), BF16)
    return pl.pallas_call(
        far_kernel,
        in_specs=[HELD] * 4,
        out_specs=[HELD] * 2,
        out_shape=[shape, shape],
        compiler_params=pltpu.CompilerParams(vmem_limit_bytes=LITTLE),
        cost_estimate=pl.CostEstimate(flops=2 << 30, bytes_accessed=6 << 20, transcendentals=0),
        name="far_product",
    )(own, other, weight, other_weight)


def near_kernel(flip, place_ref, own_ref, other_ref, weight_ref, other_weight_ref, *refs):
    outs, (held, done) = refs[:2], refs[2:]
    columns = outs[0].shape[1]
    width = columns // 2
    steps = [(b, i) for b in range(2) for i in range(2)]
    arrivals = []
    for b, i in steps:
        at = pl.ds(pl.multiple_of(place_ref[b] * columns + width * i, width), width)
        arrivals.append(
            [
                pltpu.make_async_copy(w.at[:, at], held.at[b, i, m], done.at[b, i, m])
                for m, w in enumerate((weight_ref, other_weight_ref))
            ]
        )
    for copy in sum(arrivals, []):
        copy.start()
    for (b, i), pair in zip(steps, arrivals):
        for copy in pair:
            copy.wait()
        rows = slice(ROWS, 2 * ROWS) if (b == 0) == flip else slice(0, ROWS)
        total = jnp.dot(own_ref[rows], held[b, i, 0], preferred_element_type=F32)
        total += jnp.dot(other_ref[rows], held[b, i, 1], preferred_element_type=F32)
        outs[b][:, width * i : width * i + width] = total.astype(BF16)


def near_product(own, other, out_weight, other_weight, blocks, flip):
    channels = own.shape[1]
    columns = out_weight.shape[1] // 8
    return pl.pallas_call(
        functools.partial(near_kernel, flip),
        in_specs=[SCALARS] + [HELD] * 2 + [FAR] * 2,
        out_specs=[HELD] * 2,
        out_shape=[jax.ShapeDtypeStruct((ROWS, columns), BF16)] * 2,
        scratch_shapes=[
            pltpu.VMEM((2, 2, 2, channels, columns // 2), BF16),
            pltpu.SemaphoreType.DMA((2, 2, 2)),
        ],
        compiler_params=pltpu.CompilerParams(vmem_limit_bytes=MOST),
        cost_estimate=pl.CostEstimate(flops=2 << 30, bytes_accessed=10 << 20, transcendentals=0),
        name="near_product",
    )(blocks, own, other, out_weight, other_weight)


def own_kernel(
    place_ref,
    own_ref,
    other_ref,
    weight_ref,
    other_weight_ref,
    top_more_ref,
    bottom_more_ref,
    top_ref,
    bottom_ref,
):
    total = jnp.dot(own_ref[...], weight_ref[...], preferred_element_type=F32)
    total += jnp.dot(other_ref[...], other_weight_ref[...], preferred_element_type=F32)
    top_ref[...] = total[:ROWS] + top_more_ref[...].astype(F32)
    bottom_ref[...] = total[ROWS:] + bottom_more_ref[...].astype(F32)


def own_product(own, other, out_weight, other_weight, block, top_more, bottom_more):
    rows, channels = own.shape
    columns = out_weight.shape[1] // 8
    width = 512
    steps = columns // width
    data = pl.BlockSpec((rows, channels), lambda i, at: (0, 0))
    weight = pl.BlockSpec((channels, width), lambda i, at: (0, at[0] * steps + i))
    half = pl.BlockSpec((ROWS, width), lambda i, at: (0, i))
    shape = jax.ShapeDtypeStruct((ROWS, columns), F32)
    return pl.pallas_call(
        own_kernel,
        grid_spec=pltpu.PrefetchScalarGridSpec(
            num_scalar_prefetch=1,
            grid=(steps,),
            in_specs=[data, data, weight, weight, half, half],
            out_specs=[half, half],
        ),
        out_shape=[shape, shape],
        compiler_params=pltpu.CompilerParams(vmem_limit_bytes=MOST),
        cost_estimate=pl.CostEstimate(flops=2 << 30, bytes_accessed=10 << 20, transcendentals=0),
        name="own_product",
    )(block, own, other, out_weight, other_weight, top_more, bottom_more)


def finish_kernel(top_ref, bottom_ref, top_more_ref, bottom_more_ref, out_ref):
    out_ref[:ROWS] = (top_ref[...] + top_more_ref[...].astype(F32)).astype(BF16)
    out_ref[ROWS:] = (bottom_ref[...] + bottom_more_ref[...].astype(F32)).astype(BF16)


def finish(top, bottom, top_more, bottom_more):
    columns = top.shape[1]
    width = 512
    half = pl.BlockSpec((ROWS, width), lambda i: (0, i))
    return pl.pallas_call(
        finish_kernel,
        grid=(columns // width,),
        in_specs=[half] * 4,
        out_specs=pl.BlockSpec((2 * ROWS, width), lambda i: (0, i)),
        out_shape=jax.ShapeDtypeStruct((2 * ROWS, columns), BF16),
        compiler_params=pltpu.CompilerParams(vmem_limit_bytes=MOST),
        name="finish",
    )(top, bottom, top_more, bottom_more)


def chip_shift(array, step):
    return lax.ppermute(array, "tp", [(i, (i + 2 * step) % 8) for i in range(8)])


def core_swap(array):
    return lax.ppermute(array, "tp", [(i, i ^ 1) for i in range(8)])


def block_of(step):
    place = lax.axis_index("tp")
    return 2 * ((place // 2 + step) % 4) + place % 2


def far_weights(out_weight, other_weight):
    width = out_weight.shape[1] // 8
    start = block_of(2) * width
    return [lax.dynamic_slice_in_dim(w, start, width, 1) for w in (out_weight, other_weight)]


def project(gated, out_weight, other_weight, far):
    other = core_swap(gated)
    add = lambda a, b: (a.astype(F32) + b.astype(F32)).astype(BF16)
    far_top, far_bottom = far_product(gated, other, *far)
    up = chip_shift(far_top, 1)
    down = chip_shift(far_bottom, -1)
    near = jnp.stack([block_of(1), block_of(3)])
    next_bottom, last_top = near_product(gated, other, out_weight, other_weight, near, True)
    up_direct = chip_shift(next_bottom, 1)
    down_direct = chip_shift(last_top, -1)
    next_top, last_bottom = near_product(gated, other, out_weight, other_weight, near, False)
    up_sum = chip_shift(add(next_top, up), 1)
    down_sum = chip_shift(add(last_bottom, down), -1)
    top, bottom = own_product(
        gated, other, out_weight, other_weight, block_of(0).reshape(1), down_direct, up_direct
    )
    return finish(top, bottom, up_sum, down_sum)


def convolve(key_proj, value_proj, filter_spectrum, early=()):
    first, last, forward, backward, turn, side = tables()
    as_bf16 = lambda t: jnp.asarray(t.astype(np.float32)).astype(BF16)
    turn = jnp.asarray(turn.astype(np.float32))
    side = jnp.asarray(side.astype(np.float32))
    signal = pack_signal(key_proj, value_proj)
    signal = lax.all_to_all(signal, "ctx", split_axis=0, concat_axis=0, tiled=True)
    spectrum = pack_spectrum(filter_spectrum, as_bf16(shuffles()))
    signal, spectrum = lax.optimization_barrier((signal, spectrum))
    spectrum = lax.all_to_all(spectrum, "ctx", split_axis=0, concat_axis=0, tiled=True)
    x = forward_part(signal, as_bf16(first), as_bf16(forward), turn, side)
    x, *early = lax.optimization_barrier((x, *early))
    out = filter_part(x, spectrum, as_bf16(backward), as_bf16(last), turn, side)
    return lax.all_to_all(out, "ctx", split_axis=0, concat_axis=0, tiled=True), early


def per_device(query_proj, key_proj, value_proj, filter_spectrum, skip_gain, out_weight):
    other_weight = core_swap(out_weight)
    far = far_weights(out_weight, other_weight)
    filtered, far = convolve(key_proj, value_proj, filter_spectrum, far)
    gated = gate(query_proj, key_proj, value_proj, skip_gain, filtered)
    return project(gated, out_weight, other_weight, far)


def solution(mesh):
    in_specs = (
        P("ctx", "tp"),
        P("ctx", "tp"),
        P("ctx", "tp"),
        P(None, "ctx", "tp"),
        P("tp"),
        P("tp", None),
    )
    out_specs = P("ctx", "tp")
    return jax.shard_map(
        per_device, mesh=mesh, in_specs=in_specs, out_specs=out_specs, check_vma=False
    )
```

time: 200 us -> 170 us (0.85)
  waiting for transfers between devices: 104 us -> 65.4 us
  between operations: 13.4 us -> 0.25 us
  local copies, waits for them, and re-layouts: 0.97 us -> 12 us
  starting transfers between devices: 12.7 us -> 22.3 us
  other arithmetic: 0 us -> 3.13 us
  Pallas kernels: 50.1 us -> 47.4 us
    reduce_scatter x1 -> x0, waiting for transfers between devices: 50.3 us -> none  [per_device(): out = lax.psum_scatter(terms, 'tp', scatter_dimension=0, tiled=True)]
    ppermute x0 -> x8, waiting for transfers between devices: none -> 15.7 us  [the longest x6 13 us: chip_shift(): lax.ppermute(array, 'tp', [(i, (i + 2 * step) % 8) for i in range(8)])]
    ppermute x0 -> x8, starting transfers between devices: none -> 9.56 us  [the longest x6 9.29 us: chip_shift(): lax.ppermute(array, 'tp', [(i, (i + 2 * step) % 8) for i in range(8)])]
    all_to_all x1, waiting for transfers between devices: 43.6 us -> 37 us  [convolve(): lax.all_to_all(spectrum, 'ctx', split_axis=0, concat_axis=0, tiled=True)]
    dynamic_slice x0 -> x2, local copies, waits for them, and re-layouts: none -> 6.29 us  [far_weights(): lax.dynamic_slice_in_dim(w, start, width, 1)]
    unnamed x2 -> x26, local copies, waits for them, and re-layouts: 0.97 us -> 5.69 us
    convert_element_type x0 -> x2, other arithmetic: none -> 3.06 us  [project(): add = lambda a, b: (a.astype(F32) + b.astype(F32)).astype(BF16)]
    all_to_all x1, waiting for transfers between devices: 9.78 us -> 12.8 us  [convolve(): lax.all_to_all(signal, 'ctx', split_axis=0, concat_axis=0, tiled=True)]
  transfers between devices with their start and end apart: 3 -> 10, of which waited for: 3 -> 7; matrix products, arithmetic and copies ran while one was open for 0% -> 6% of each run, Pallas kernels for 9% -> 17%
where the time goes in v2:
time: 170 us; the launch traced here: 169 us
  waiting for transfers between devices  65.4 us (38%)
  Pallas kernels  47.4 us (28%)
  starting transfers between devices  22.3 us (13%)
  blocking collectives  19 us (11%)
  local copies, waits for them, and re-layouts  12 us (7%)
  other arithmetic  3.13 us (2%)
    all_to_all x1, waiting for transfers between devices, convolve(): lax.all_to_all(spectrum, 'ctx', split_axis=0, concat_axis=0, tiled=True)  37 us
    all_to_all x1, blocking collectives, convolve(): lax.all_to_all(out, 'ctx', split_axis=0, concat_axis=0, tiled=True)  19 us
    ppermute x6, waiting for transfers between devices, chip_shift(): lax.ppermute(array, 'tp', [(i, (i + 2 * step) % 8) for i in range(8)])  13 us
    all_to_all x1, waiting for transfers between devices, convolve(): lax.all_to_all(signal, 'ctx', split_axis=0, concat_axis=0, tiled=True)  12.8 us
    pallas_call x1, Pallas kernels, filter_part(): pl.pallas_call(filter_kernel, in_specs=[FAR] * 4 + [HELD] * 2, out_specs=...  11.7 us
    pallas_call x2, Pallas kernels, near_product(): pl.pallas_call(functools.partial(near_kernel, flip), in_specs=[SCALARS] +...  10.8 us
    pallas_call x1, Pallas kernels, forward_part(): pl.pallas_call(forward_kernel, in_specs=[HELD] * 5, out_specs=HELD, out_s...  9.93 us
    ppermute x6, starting transfers between devices, chip_shift(): lax.ppermute(array, 'tp', [(i, (i + 2 * step) % 8) for i in range(8)])  9.29 us
  transfers between devices with their start and end apart: 10, of which 7 were waited for; matrix products, arithmetic and copies ran while one was open for 6% of the time, Pallas kernels for 17%

profile of v2, /device:TPU:0, one launch (start us, length us, event | category | flops | bytes accessed | tf_op | source)
XLA Modules:
  0.0 169.5 jit_solution(98808921717466310)
XLA Ops:
  0.0 0.0 copy-start.11
  0.0 0.0 collective-permute-start
  0.0 3.0 %pack_signal.1 = bf16[16,256,128]{2,1,0:T(8,128)(2,1)} custom-call(bf16[512,1024]{1,0:T(8,128)(2,1)} %key_ref.3, bf16[512,1024]{1,0:T(8,128)(2,1)} %value_ref.3), custom_call_target="tpu_custom_call" | custom-call | flops 1048576 | bytes 3145728 | tf_op jit(solution)/shard_map/pack_signal/pallas_call | solution.py:97
  3.0 8.1 %all-to-all-start = ((bf16[16,256,128]{2,1,0:T(8,128)(2,1)}), bf16[16,256,128]{2,1,0:T(8,128)(2,1)S(1)}, u32[]{:S(2)}, u32[]{:S(2)}) async-start(bf16[16,256,128]{2,1,0:T(8,128)(2,1)} %pack_signal.1), calls=%async_computation | async-start | bytes 2097152 | tf_op jit(solution)/shard_map/all_to_all | solution.py:525
  11.1 0.0 copy-done.11
  11.1 0.0 copy-start.2
  11.1 2.2 %copy-done.2 = bf16[2,1024,1024]{2,1,0:T(8,128)(2,1)S(1)} copy-done((bf16[2,1024,1024]{2,1,0:T(8,128)(2,1)S(1)}, bf16[2,1024,1024]{2,1,0:T(8,128)(2,1)}, u32[]{:S(2)}) %copy-start.2) | copy-done | bytes 4194328
  13.3 1.4 pack_spectrum.1
  14.8 0.0 copy-start
  14.8 2.0 %copy-done = bf16[16,2,32,16,128]{4,3,2,1,0:T(8,128)(2,1)} copy-done((bf16[16,2,32,16,128]{4,3,2,1,0:T(8,128)(2,1)}, bf16[16,2,32,16,128]{4,3,2,1,0:T(8,128)(2,1)S(1)}, u32[]{:S(2)}) %copy-start) | copy-done | bytes 4194328
  16.8 12.8 %all-to-all-done.signal_ref = bf16[16,256,128]{2,1,0:T(8,128)(2,1)S(1)} async-done(((bf16[16,256,128]{2,1,0:T(8,128)(2,1)}), bf16[16,256,128]{2,1,0:T(8,128)(2,1)S(1)}, u32[]{:S(2)}, u32[]{:S(2)}) %all-to-all-start) | async-done | bytes 1048608 | tf_op jit(solution)/shard_map/all_to_all | solution.py:525
  29.6 4.5 %all-to-all-start.1 = ((bf16[16,2,32,16,128]{4,3,2,1,0:T(8,128)(2,1)}), bf16[16,2,32,16,128]{4,3,2,1,0:T(8,128)(2,1)}, u32[]{:S(2)}, u32[]{:S(2)}) async-start(bf16[16,2,32,16,128]{4,3,2,1,0:T(8,128)(2,1)} %copy-done), calls=%async_computation.1 | async-start | bytes 8388608 | tf_op jit(solution)/shard_map/all_to_all | solution.py:528
  34.1 0.0 copy-start.7
  34.1 0.0 copy-start.9
  34.1 0.0 copy-start.10
  34.2 3.2 %constant_dynamic-slice_fusion.1.weight_ref = bf16[1024,1024]{1,0:T(8,128)(2,1)} fusion(bf16[1024,8192]{1,0:T(8,128)(2,1)} %weight_ref.5, s32[]{:T(128)S(6)} %select_n.44), kind=kLoop, calls=%fused_computation.4 | loop fusion | bytes 4194308 | tf_op jit(solution)/shard_map/dynamic_slice | solution.py:497
  37.4 0.0 copy-done.7
  37.4 0.0 copy-done.9
  37.4 0.0 copy-done.10
  37.4 9.9 %forward_part.1.x_ref = bf16[17,2,256,128]{3,2,1,0:T(8,128)(2,1)S(1)} custom-call(bf16[512,256]{1,0:T(8,128)(2,1)S(1)} %copy-done.10, bf16[512,512]{1,0:T(8,128)(2,1)S(1)} %copy-done.9, f32[17,2,256,128]{3,2,1,0:T(8,128)} %constant.83.clone.turn_ref.turn_from, f32[2,256,128]{2,1,0:T(8,128)S(1)} %copy-done.7, bf16[16,256,128]{2,1,0:T(8,128)(2,1)S(1)} %all-to-all-done.signal_ref), custom_call_target="tpu_custom_call" | custom-call | flops 2147483648 | bytes 12582912 | tf_op jit(solution)/shard_map/forward_part/pallas_call | solution.py:197
  47.3 0.0 copy-start.1
  47.4 1.4 copy-done.1
  48.8 0.0 collective-permute-done.other_weight_ref
  48.8 3.1 %constant_dynamic-slice_fusion.other_weight_ref = bf16[1024,1024]{1,0:T(8,128)(2,1)} fusion(bf16[1024,8192]{1,0:T(8,128)(2,1)} %collective-permute-done.other_weight_ref, s32[]{:T(128)S(6)} %select_n.44), kind=kLoop, calls=%fused_computation.3 | loop fusion | bytes 4194308 | tf_op jit(solution)/shard_map/dynamic_slice | solution.py:497
  51.9 0.0 copy-start.3
  51.9 0.0 copy-start.4
  51.9 0.0 copy-start.12
  51.9 37.0 %all-to-all-done.1.spec_ref = bf16[16,2,32,16,128]{4,3,2,1,0:T(8,128)(2,1)} async-done(((bf16[16,2,32,16,128]{4,3,2,1,0:T(8,128)(2,1)}), bf16[16,2,32,16,128]{4,3,2,1,0:T(8,128)(2,1)}, u32[]{:S(2)}, u32[]{:S(2)}) %all-to-all-start.1) | async-done | bytes 4194336 | tf_op jit(solution)/shard_map/all_to_all | solution.py:528
  88.9 0.0 copy-start.8
  88.9 11.7 %filter_part.1 = bf16[16,256,128]{2,1,0:T(8,128)(2,1)} custom-call(bf16[512,512]{1,0:T(8,128)(2,1)} %constant.90.backward_from, bf16[256,512]{1,0:T(8,128)(2,1)} %constant.91.last_from, f32[2,256,128]{2,1,0:T(8,128)} %constant.84.clone.side_ref.side_from, f32[17,2,256,128]{3,2,1,0:T(8,128)} %constant.83.clone.turn_ref.turn_from, ...), custom_call_target="tpu_custom_call" | custom-call | flops 2147483648 | bytes 16777216 | tf_op jit(solution)/shard_map/filter_part/pallas_call | solution.py:305
  100.6 0.0 copy-start.5
  100.6 0.0 copy-start.6
  100.6 19.0 %all_to_all.15.filtered_ref = bf16[16,256,128]{2,1,0:T(8,128)(2,1)S(1)} all-to-all(bf16[16,256,128]{2,1,0:T(8,128)(2,1)} %filter_part.1), channel_id=1, replica_groups=mesh['ctx'=16,'tp'=8] {'ctx'}, dimensions={0} | all-to-all | bytes 2097152 | tf_op jit(solution)/shard_map/all_to_all | solution.py:532
  119.6 0.0 copy-done.3
  119.6 0.0 copy-done.4
  119.6 0.0 copy-done.12
  119.6 0.0 copy-done.8
  119.7 1.0 gate.1.own_ref
  120.6 0.3 collective-permute-start.1
  120.9 2.6 %collective-permute-done.1.other_ref = bf16[512,1024]{1,0:T(8,128)(2,1)S(1)} collective-permute-done((bf16[512,1024]{1,0:T(8,128)(2,1)S(1)}, bf16[512,1024]{1,0:T(8,128)(2,1)S(1)}, u32[]{:S(2)}, u32[]{:S(2)}) %collective-permute-start.1) | collective-permute-done | bytes 1048608 | tf_op jit(solution)/shard_map/ppermute | solution.py:486
  123.6 0.0 copy-done.5
  123.6 0.0 copy-done.6
  123.6 3.2 %far_product.1 = (bf16[256,1024]{1,0:T(8,128)(2,1)}, bf16[256,1024]{1,0:T(8,128)(2,1)}) custom-call(bf16[512,1024]{1,0:T(8,128)(2,1)S(1)} %gate.1.own_ref, bf16[512,1024]{1,0:T(8,128)(2,1)S(1)} %collective-permute-done.1.other_ref, bf16[1024,1024]{1,0:T(8,128)(2,1)S(1)} %copy-done.5, bf16[1024,1024]{1,0:T(8,128)(2,1)S(1)} %copy-done.6), custom_call_target="tpu_custom_call" | custom-call | flops 2147483648 | bytes 6291456 | tf_op jit(solution)/shard_map/far_product/pallas_call | solution.py:366
  126.8 2.8 %collective-permute-start.6 = (bf16[256,1024]{1,0:T(8,128)(2,1)}, bf16[256,1024]{1,0:T(8,128)(2,1)}, u32[]{:S(2)}, u32[]{:S(2)}) collective-permute-start(bf16[256,1024]{1,0:T(8,128)(2,1)} %get-tuple-element.30), channel_id=1, source_target_pairs={{0,6},{1,7},{2,0},{3,1},{4,2},{5,3},{6,4},{7,5},{8,14},{9,15},{10,... | collective-permute-start | bytes 1572872 | tf_op jit(solution)/shard_map/ppermute | solution.py:482
  129.6 0.1 pad_add_fusion.place_ref
  129.6 0.0 collective-permute-start.4
  129.6 5.8 %near_product.2 = (bf16[256,1024]{1,0:T(8,128)(2,1)}, bf16[256,1024]{1,0:T(8,128)(2,1)}) custom-call(s32[2]{0:T(128)S(1)} %pad_add_fusion.place_ref, bf16[512,1024]{1,0:T(8,128)(2,1)S(1)} %gate.1.own_ref, bf16[512,1024]{1,0:T(8,128)(2,1)S(1)} %collective-permute-done.1.other_ref, bf16[1024,8192]{1,0:T(8,128)(2,1)} %weight_ref.5, ...), custom_call_target="tpu_custom_call" | custom-call | flops 2147483648 | bytes 10485760 | tf_op jit(solution)/shard_map/near_product/pallas_call | solution.py:405
  135.4 3.3 %collective-permute-start.2 = (bf16[256,1024]{1,0:T(8,128)(2,1)}, bf16[256,1024]{1,0:T(8,128)(2,1)S(1)}, u32[]{:S(2)}, u32[]{:S(2)}) collective-permute-start(bf16[256,1024]{1,0:T(8,128)(2,1)} %get-tuple-element.21), channel_id=1, source_target_pairs={{0,6},{1,7},{2,0},{3,1},{4,2},{5,3},{6,4},{7,5},{8,14},{9,15},{10,... | collective-permute-start | bytes 1572872 | tf_op jit(solution)/shard_map/ppermute | solution.py:482
  138.7 0.0 collective-permute-start.3
  138.7 5.0 %near_product.3 = (bf16[256,1024]{1,0:T(8,128)(2,1)S(1)}, bf16[256,1024]{1,0:T(8,128)(2,1)S(1)}) custom-call(s32[2]{0:T(128)S(1)} %pad_add_fusion.place_ref, bf16[512,1024]{1,0:T(8,128)(2,1)S(1)} %gate.1.own_ref, bf16[512,1024]{1,0:T(8,128)(2,1)S(1)} %collective-permute-done.1.other_ref, bf16[1024,8192]{1,0:T(8,128)(2,1)} %weight_ref.5, ...), custom_call_target="tpu_custom_call" | custom-call | flops 2147483648 | bytes 10485760 | tf_op jit(solution)/shard_map/near_product/pallas_call | solution.py:405
  143.7 0.0 collective-permute-done.6
  143.8 2.0 %add_convert_fusion = bf16[256,1024]{1,0:T(8,128)(2,1)} fusion(bf16[256,1024]{1,0:T(8,128)(2,1)} %collective-permute-done.6, bf16[256,1024]{1,0:T(8,128)(2,1)S(1)} %get-tuple-element.29), kind=kLoop, calls=%fused_computation | loop fusion | flops 1048576 | bytes 1572864 | tf_op jit(solution)/shard_map/convert_element_type | solution.py:502
  145.8 3.2 %collective-permute-start.7 = (bf16[256,1024]{1,0:T(8,128)(2,1)}, bf16[256,1024]{1,0:T(8,128)(2,1)}, u32[]{:S(2)}, u32[]{:S(2)}) collective-permute-start(bf16[256,1024]{1,0:T(8,128)(2,1)} %add_convert_fusion), channel_id=1, source_target_pairs={{0,6},{1,7},{2,0},{3,1},{4,2},{5,3},{6,4},{7,5},{8,14},{9,15},{10,... | collective-permute-start | bytes 1572872 | tf_op jit(solution)/shard_map/ppermute | solution.py:482
  149.0 0.0 collective-permute-done.4
  149.0 1.0 add_convert_fusion.1
  150.1 0.0 collective-permute-start.5
  150.1 3.3 %collective-permute-done.2.top_more_ref = bf16[256,1024]{1,0:T(8,128)(2,1)S(1)} collective-permute-done((bf16[256,1024]{1,0:T(8,128)(2,1)}, bf16[256,1024]{1,0:T(8,128)(2,1)S(1)}, u32[]{:S(2)}, u32[]{:S(2)}) %collective-permute-start.2) | collective-permute-done | bytes 524320 | tf_op jit(solution)/shard_map/ppermute | solution.py:482
  153.4 3.7 %collective-permute-done.3.bottom_more_ref = bf16[256,1024]{1,0:T(8,128)(2,1)S(1)} collective-permute-done((bf16[256,1024]{1,0:T(8,128)(2,1)}, bf16[256,1024]{1,0:T(8,128)(2,1)S(1)}, u32[]{:S(2)}, u32[]{:S(2)}) %collective-permute-start.3) | collective-permute-done | bytes 524320 | tf_op jit(solution)/shard_map/ppermute | solution.py:482
  157.1 4.2 %own_product.1 = (f32[256,1024]{1,0:T(8,128)S(1)}, f32[256,1024]{1,0:T(8,128)S(1)}) custom-call(s32[1]{0:T(128)} %bitcast.place_ref, bf16[512,1024]{1,0:T(8,128)(2,1)S(1)} %gate.1.own_ref, bf16[512,1024]{1,0:T(8,128)(2,1)S(1)} %collective-permute-done.1.other_ref, bf16[1024,8192]{1,0:T(8,128)(2,1)} %weight_ref.5, ...), custom_call_target="tpu_custom_call" | custom-call | flops 2147483648 | bytes 10485760 | tf_op jit(solution)/shard_map/own_product/pallas_call | solution.py:446
  161.3 2.5 %collective-permute-done.7.bottom_more_ref = bf16[256,1024]{1,0:T(8,128)(2,1)} collective-permute-done((bf16[256,1024]{1,0:T(8,128)(2,1)}, bf16[256,1024]{1,0:T(8,128)(2,1)}, u32[]{:S(2)}, u32[]{:S(2)}) %collective-permute-start.7) | collective-permute-done | bytes 524320 | tf_op jit(solution)/shard_map/ppermute | solution.py:482
  163.8 3.5 %collective-permute-done.5.top_more_ref = bf16[256,1024]{1,0:T(8,128)(2,1)} collective-permute-done((bf16[256,1024]{1,0:T(8,128)(2,1)}, bf16[256,1024]{1,0:T(8,128)(2,1)}, u32[]{:S(2)}, u32[]{:S(2)}) %collective-permute-start.5) | collective-permute-done | bytes 524320 | tf_op jit(solution)/shard_map/ppermute | solution.py:482
  167.3 2.2 %finish.1 = bf16[512,1024]{1,0:T(8,128)(2,1)} custom-call(f32[256,1024]{1,0:T(8,128)S(1)} %get-tuple-element.23.top_ref, f32[256,1024]{1,0:T(8,128)S(1)} %get-tuple-element.24.bottom_ref, bf16[256,1024]{1,0:T(8,128)(2,1)} %collective-permute-done.5.top_more_ref, bf16[256,1024]{1,0:T(8,128)(2,1)} %collective-permute-done.7.bottom_more_ref), custom_call_target="tpu_custom_call" | custom-call | tf_op jit(solution)/shard_map/finish/pallas_call | solution.py:470
Async XLA Ops:
  0.0 11.1 %copy-start.11 = (bf16[2,256,256]{2,1,0:T(8,128)(2,1)S(1)}, bf16[2,256,256]{2,1,0:T(8,128)(2,1)}, u32[]{:S(2)}) copy-start(bf16[2,256,256]{2,1,0:T(8,128)(2,1)} %constant.94.shuffle_ref) | copy-start | bytes 786436
  0.0 48.8 %collective-permute-start = (bf16[1024,8192]{1,0:T(8,128)(2,1)}, bf16[1024,8192]{1,0:T(8,128)(2,1)}, u32[]{:S(2)}, u32[]{:S(2)}) collective-permute-start(bf16[1024,8192]{1,0:T(8,128)(2,1)} %weight_ref.5), channel_id=1, source_target_pairs={{0,1},{1,0},{2,3},{3,2},{4,5},{5,4},{6,7},{7,6},{8,9},{9,8},{10,11... | collective-permute-start | bytes 50331656 | tf_op jit(solution)/shard_map/ppermute | solution.py:486
  3.0 26.6 %all-to-all-start = ((bf16[16,256,128]{2,1,0:T(8,128)(2,1)}), bf16[16,256,128]{2,1,0:T(8,128)(2,1)S(1)}, u32[]{:S(2)}, u32[]{:S(2)}) async-start(bf16[16,256,128]{2,1,0:T(8,128)(2,1)} %pack_signal.1), calls=%async_computation | async-start | bytes 2097152 | tf_op jit(solution)/shard_map/all_to_all | solution.py:525
  11.1 2.2 %copy-start.2 = (bf16[2,1024,1024]{2,1,0:T(8,128)(2,1)S(1)}, bf16[2,1024,1024]{2,1,0:T(8,128)(2,1)}, u32[]{:S(2)}) copy-start(bf16[2,1024,1024]{2,1,0:T(8,128)(2,1)} %spec_ref.1) | copy-start | bytes 12582916
  14.8 2.0 %copy-start = (bf16[16,2,32,16,128]{4,3,2,1,0:T(8,128)(2,1)}, bf16[16,2,32,16,128]{4,3,2,1,0:T(8,128)(2,1)S(1)}, u32[]{:S(2)}) copy-start(bf16[16,2,32,16,128]{4,3,2,1,0:T(8,128)(2,1)S(1)} %pack_spectrum.1) | copy-start | bytes 12582916
  29.6 59.4 %all-to-all-start.1 = ((bf16[16,2,32,16,128]{4,3,2,1,0:T(8,128)(2,1)}), bf16[16,2,32,16,128]{4,3,2,1,0:T(8,128)(2,1)}, u32[]{:S(2)}, u32[]{:S(2)}) async-start(bf16[16,2,32,16,128]{4,3,2,1,0:T(8,128)(2,1)} %copy-done), calls=%async_computation.1 | async-start | bytes 8388608 | tf_op jit(solution)/shard_map/all_to_all | solution.py:528
  34.1 3.3 %copy-start.7 = (f32[2,256,128]{2,1,0:T(8,128)S(1)}, f32[2,256,128]{2,1,0:T(8,128)}, u32[]{:S(2)}) copy-start(f32[2,256,128]{2,1,0:T(8,128)} %constant.84.clone.side_ref.side_from) | copy-start | bytes 786436
  34.1 3.3 %copy-start.9 = (bf16[512,512]{1,0:T(8,128)(2,1)S(1)}, bf16[512,512]{1,0:T(8,128)(2,1)}, u32[]{:S(2)}) copy-start(bf16[512,512]{1,0:T(8,128)(2,1)} %constant.93.forward_ref) | copy-start | bytes 1572868
  34.1 3.3 %copy-start.10 = (bf16[512,256]{1,0:T(8,128)(2,1)S(1)}, bf16[512,256]{1,0:T(8,128)(2,1)}, u32[]{:S(2)}) copy-start(bf16[512,256]{1,0:T(8,128)(2,1)} %constant.92.first_ref) | copy-start | bytes 786436
  47.3 1.4 copy-start.1
  51.9 67.8 %copy-start.3 = (bf16[512,1024]{1,0:T(8,128)(2,1)S(1)}, bf16[512,1024]{1,0:T(8,128)(2,1)}, u32[]{:S(2)}) copy-start(bf16[512,1024]{1,0:T(8,128)(2,1)} %key_ref.3) | copy-start | bytes 3145732
  51.9 67.8 %copy-start.4 = (bf16[512,1024]{1,0:T(8,128)(2,1)S(1)}, bf16[512,1024]{1,0:T(8,128)(2,1)}, u32[]{:S(2)}) copy-start(bf16[512,1024]{1,0:T(8,128)(2,1)} %value_ref.3) | copy-start | bytes 3145732
  51.9 67.8 %copy-start.12 = (f32[1024]{0:T(1024)S(1)}, f32[1024]{0:T(1024)}, u32[]{:S(2)}) copy-start(f32[1024]{0:T(1024)} %param.17) | copy-start | bytes 12292
  88.9 30.7 %copy-start.8 = (bf16[512,1024]{1,0:T(8,128)(2,1)S(1)}, bf16[512,1024]{1,0:T(8,128)(2,1)}, u32[]{:S(2)}) copy-start(bf16[512,1024]{1,0:T(8,128)(2,1)} %query_ref.1) | copy-start | bytes 3145732
  100.6 23.0 %copy-start.5 = (bf16[1024,1024]{1,0:T(8,128)(2,1)S(1)}, bf16[1024,1024]{1,0:T(8,128)(2,1)}, u32[]{:S(2)}) copy-start(bf16[1024,1024]{1,0:T(8,128)(2,1)} %constant_dynamic-slice_fusion.1.weight_ref) | copy-start | bytes 6291460
  100.6 22.9 %copy-start.6 = (bf16[1024,1024]{1,0:T(8,128)(2,1)S(1)}, bf16[1024,1024]{1,0:T(8,128)(2,1)}, u32[]{:S(2)}) copy-start(bf16[1024,1024]{1,0:T(8,128)(2,1)} %constant_dynamic-slice_fusion.other_weight_ref) | copy-start | bytes 6291460
  120.6 2.9 %collective-permute-start.1 = (bf16[512,1024]{1,0:T(8,128)(2,1)S(1)}, bf16[512,1024]{1,0:T(8,128)(2,1)S(1)}, u32[]{:S(2)}, u32[]{:S(2)}) collective-permute-start(bf16[512,1024]{1,0:T(8,128)(2,1)S(1)} %gate.1.own_ref), channel_id=1, source_target_pairs={{0,1},{1,0},{2,3},{3,2},{4,5},{5,4},{6,7},{7,6},{8,9},{9,8},{10,11... | collective-permute-start | bytes 3145736 | tf_op jit(solution)/shard_map/ppermute | solution.py:486
  126.8 17.0 %collective-permute-start.6 = (bf16[256,1024]{1,0:T(8,128)(2,1)}, bf16[256,1024]{1,0:T(8,128)(2,1)}, u32[]{:S(2)}, u32[]{:S(2)}) collective-permute-start(bf16[256,1024]{1,0:T(8,128)(2,1)} %get-tuple-element.30), channel_id=1, source_target_pairs={{0,6},{1,7},{2,0},{3,1},{4,2},{5,3},{6,4},{7,5},{8,14},{9,15},{10,... | collective-permute-start | bytes 1572872 | tf_op jit(solution)/shard_map/ppermute | solution.py:482
  129.6 19.4 %collective-permute-start.4 = (bf16[256,1024]{1,0:T(8,128)(2,1)}, bf16[256,1024]{1,0:T(8,128)(2,1)S(1)}, u32[]{:S(2)}, u32[]{:S(2)}) collective-permute-start(bf16[256,1024]{1,0:T(8,128)(2,1)} %get-tuple-element.28), channel_id=1, source_target_pairs={{0,2},{1,3},{2,4},{3,5},{4,6},{5,7},{6,0},{7,1},{8,10},{9,11},{10,... | collective-permute-start | bytes 1572872 | tf_op jit(solution)/shard_map/ppermute | solution.py:482
  135.4 17.9 %collective-permute-start.2 = (bf16[256,1024]{1,0:T(8,128)(2,1)}, bf16[256,1024]{1,0:T(8,128)(2,1)S(1)}, u32[]{:S(2)}, u32[]{:S(2)}) collective-permute-start(bf16[256,1024]{1,0:T(8,128)(2,1)} %get-tuple-element.21), channel_id=1, source_target_pairs={{0,6},{1,7},{2,0},{3,1},{4,2},{5,3},{6,4},{7,5},{8,14},{9,15},{10,... | collective-permute-start | bytes 1572872 | tf_op jit(solution)/shard_map/ppermute | solution.py:482
  138.7 18.4 %collective-permute-start.3 = (bf16[256,1024]{1,0:T(8,128)(2,1)}, bf16[256,1024]{1,0:T(8,128)(2,1)S(1)}, u32[]{:S(2)}, u32[]{:S(2)}) collective-permute-start(bf16[256,1024]{1,0:T(8,128)(2,1)} %get-tuple-element.22), channel_id=1, source_target_pairs={{0,2},{1,3},{2,4},{3,5},{4,6},{5,7},{6,0},{7,1},{8,10},{9,11},{10,... | collective-permute-start | bytes 1572872 | tf_op jit(solution)/shard_map/ppermute | solution.py:482
  145.8 18.0 %collective-permute-start.7 = (bf16[256,1024]{1,0:T(8,128)(2,1)}, bf16[256,1024]{1,0:T(8,128)(2,1)}, u32[]{:S(2)}, u32[]{:S(2)}) collective-permute-start(bf16[256,1024]{1,0:T(8,128)(2,1)} %add_convert_fusion), channel_id=1, source_target_pairs={{0,6},{1,7},{2,0},{3,1},{4,2},{5,3},{6,4},{7,5},{8,14},{9,15},{10,... | collective-permute-start | bytes 1572872 | tf_op jit(solution)/shard_map/ppermute | solution.py:482
  150.1 17.3 %collective-permute-start.5 = (bf16[256,1024]{1,0:T(8,128)(2,1)}, bf16[256,1024]{1,0:T(8,128)(2,1)}, u32[]{:S(2)}, u32[]{:S(2)}) collective-permute-start(bf16[256,1024]{1,0:T(8,128)(2,1)} %add_convert_fusion.1), channel_id=1, source_target_pairs={{0,2},{1,3},{2,4},{3,5},{4,6},{5,7},{6,0},{7,1},{8,10},{9,11},{10,... | collective-permute-start | bytes 1572872 | tf_op jit(solution)/shard_map/ppermute | solution.py:482

commit v3 on v2

--- a/solution.py
+++ b/solution.py
@@ -1,4 +1,5 @@
 import functools
+import math
 
 import numpy as np
 
@@ -16,7 +17,7 @@
 SCALARS = pl.BlockSpec(memory_space=pltpu.SMEM)
 F32 = jnp.float32
 BF16 = jnp.bfloat16
-TIGHT = 56 * 1024 * 1024
+TIGHT = 46 * 1024 * 1024
 BIG = 60 * 1024 * 1024
 LITTLE = 24 * 1024 * 1024
 MOST = 48 * 1024 * 1024
@@ -97,6 +98,7 @@
     return pl.pallas_call(
         pack_signal_kernel,
         in_specs=[FAR] * 2,
+        out_specs=HELD,
         out_shape=jax.ShapeDtypeStruct((16, ROWS, 128), BF16),
         scratch_shapes=[
             pltpu.VMEM(key_proj.shape, BF16),
@@ -153,7 +155,8 @@
     return jnp.where(low_lanes(shape), 1.0, -1.0).astype(F32)
 
 
-def forward_kernel(first_ref, forward_ref, turn_ref, side_ref, signal_ref, out_ref, part):
+def forward_kernel(first_ref, forward_ref, turn_ref, signal_ref, out_ref, part):
+    side_ref = turn_ref.at[HALF]
     sign = sign_lanes((16, 128))
 
     def step(q, carry):
@@ -193,50 +196,45 @@
     out_ref[16] = x.astype(BF16).reshape(2, ROWS, 128)
 
 
-def forward_part(signal, first, forward, turn, side):
+def forward_part(signal, first, forward, turn):
     return pl.pallas_call(
         forward_kernel,
-        in_specs=[HELD] * 5,
+        in_specs=[HELD] * 4,
         out_specs=HELD,
         out_shape=jax.ShapeDtypeStruct((HALF, 2, ROWS, 128), BF16),
         scratch_shapes=[pltpu.VMEM((HALF, 2, ROWS, 128), BF16)],
         compiler_params=pltpu.CompilerParams(vmem_limit_bytes=MOST),
         cost_estimate=pl.CostEstimate(flops=2 << 30, bytes_accessed=12 << 20, transcendentals=0),
         name="forward_part",
-    )(first, forward, turn, side, signal)
+    )(first, forward, turn, signal)
 
 
 def filter_kernel(
-    backward_from,
-    last_from,
-    side_from,
-    turn_from,
+    tables_from,
+    waves_from,
     x_ref,
     spec_ref,
     out_ref,
-    backward_ref,
-    last_ref,
-    side_ref,
-    turn_ref,
+    tables_ref,
+    waves_ref,
     held,
     products,
     sums,
     table_done,
-    turn_done,
 ):
-    tables = [
-        pltpu.make_async_copy(source, target, table_done.at[n])
-        for n, (source, target) in enumerate(
-            ((backward_from, backward_ref), (side_from, side_ref), (last_from, last_ref))
+    backward_ref = tables_ref.at[: 2 * ROWS]
+    last_ref = tables_ref.at[2 * ROWS :]
+    copies = [
+        pltpu.make_async_copy(source.at[some], target.at[some], table_done.at[n])
+        for n, (source, target, some) in enumerate(
+            (
+                (tables_from, tables_ref, pl.ds(0, 2 * ROWS)),
+                (waves_from, waves_ref, pl.ds(0, HALF + 16)),
+                (tables_from, tables_ref, pl.ds(2 * ROWS, ROWS)),
+            )
         )
     ]
-    turns = []
-    for g in range(9):
-        some = pl.ds(2 * g, 2 if g < 8 else 1)
-        turns.append(
-            pltpu.make_async_copy(turn_from.at[some], turn_ref.at[some], turn_done.at[g])
-        )
-    for copy in tables[:2] + turns + tables[2:]:
+    for copy in copies:
         copy.start()
     sign = sign_lanes((16, 128))
 
@@ -265,31 +263,34 @@
                 products[start // 2, below, lanes] = (x_re * h_im + x_im * h_re).astype(BF16)
         wide = 128 * len(group)
         if start == 0:
-            tables[0].wait()
+            copies[0].wait()
         sums[start // 2, :, :wide] = jnp.dot(
             backward_ref[...], products[start // 2, :, :wide], preferred_element_type=F32
         )
         if start == 0:
-            tables[1].wait()
-        turns[start // 2].wait()
+            copies[1].wait()
         for n, e in enumerate(group):
+            base_re, base_im = waves_ref[e, 0], waves_ref[e, 1]
             lanes = slice(128 * n, 128 * n + 128)
             for j in range(16):
                 rows = slice(16 * j, 16 * j + 16)
                 below = slice(ROWS + 16 * j, ROWS + 16 * j + 16)
                 b_re = sums[start // 2, rows, lanes]
                 b_im = sums[start // 2, below, lanes]
-                side_re, side_im = side_ref[0, rows], side_ref[1, rows]
+                side_re, side_im = waves_ref[HALF + j, 0], waves_ref[HALF + j, 1]
                 s_re = b_re * side_re + b_im * side_im
                 s_im = b_im * side_re - b_re * side_im
                 c_re = s_re * sign + pltpu.roll(s_re, 64, 1)
                 c_im = s_im * sign + pltpu.roll(s_im, 64, 1)
-                cos, sin = turn_ref[e, 0, rows], turn_ref[e, 1, rows]
+                angle = 2.0 * math.pi * (16 * j * e % 16384) / 16384.0
+                step_re, step_im = math.cos(angle), -math.sin(angle)
+                cos = base_re * step_re - base_im * step_im
+                sin = base_re * step_im + base_im * step_re
                 held[e, rows] = (c_re * cos + c_im * sin).astype(BF16)
                 if e not in (0, 16):
                     held[16 + e, rows] = (c_im * cos - c_re * sin).astype(BF16)
 
-    tables[2].wait()
+    copies[2].wait()
     for q in range(0, 16, 2):
         block = jnp.concatenate(
             [held[:, 16 * p : 16 * p + 16].reshape(512, 128) for p in (q, q + 1)], axis=1
@@ -301,24 +302,23 @@
             )
 
 
-def filter_part(x, spectrum, backward, last, turn, side):
+def filter_part(x, spectrum, tables, waves):
     return pl.pallas_call(
         filter_kernel,
-        in_specs=[FAR] * 4 + [HELD] * 2,
+        in_specs=[FAR] * 2 + [HELD] * 2,
         out_specs=HELD,
         out_shape=jax.ShapeDtypeStruct((16, ROWS, 128), BF16),
         scratch_shapes=[
-            *[pltpu.VMEM(t.shape, t.dtype) for t in (backward, last, side, turn)],
+            *[pltpu.VMEM(t.shape, t.dtype) for t in (tables, waves)],
             pltpu.VMEM((32, ROWS, 128), BF16),
             pltpu.VMEM((9, 2 * ROWS, 256), BF16),
             pltpu.VMEM((9, 2 * ROWS, 256), F32),
             pltpu.SemaphoreType.DMA((3,)),
-            pltpu.SemaphoreType.DMA((9,)),
         ],
         compiler_params=pltpu.CompilerParams(vmem_limit_bytes=TIGHT),
         cost_estimate=pl.CostEstimate(flops=2 << 30, bytes_accessed=16 << 20, transcendentals=0),
         name="filter_part",
-    )(backward, last, side, turn, x, spectrum)
+    )(tables, waves, x, spectrum)
 
 
 def gate_kernel(query_ref, key_ref, value_ref, skip_ref, filtered_ref, out_ref):
@@ -351,31 +351,47 @@
     )(query_proj, key_proj, value_proj, skip_gain.reshape(1, channels), filtered)
 
 
-def far_kernel(own_ref, other_ref, weight_ref, other_weight_ref, top_ref, bottom_ref):
+def far_own_kernel(own_ref, weight_ref, out_ref):
+    out_ref[...] = jnp.dot(own_ref[...], weight_ref[...], preferred_element_type=F32)
+
+
+def far_kernel(own_ref, other_ref, weight_ref, top_ref, bottom_ref):
     width = 256
     for start in range(0, weight_ref.shape[1], width):
         lanes = slice(start, start + width)
-        total = jnp.dot(own_ref[...], weight_ref[:, lanes], preferred_element_type=F32)
-        total += jnp.dot(other_ref[...], other_weight_ref[:, lanes], preferred_element_type=F32)
+        total = own_ref[:, lanes]
+        total += jnp.dot(other_ref[...], weight_ref[:, lanes], preferred_element_type=F32)
         top_ref[:, lanes] = total[:ROWS].astype(BF16)
         bottom_ref[:, lanes] = total[ROWS:].astype(BF16)
 
 
-def far_product(own, other, weight, other_weight):
+def far_own_product(own, weight):
+    return pl.pallas_call(
+        far_own_kernel,
+        in_specs=[HELD] * 2,
+        out_specs=HELD,
+        out_shape=jax.ShapeDtypeStruct((own.shape[0], weight.shape[1]), F32),
+        compiler_params=pltpu.CompilerParams(vmem_limit_bytes=LITTLE),
+        cost_estimate=pl.CostEstimate(flops=1 << 30, bytes_accessed=5 << 20, transcendentals=0),
+        name="far_own_product",
+    )(own, weight)
+
+
+def far_product(own, other, weight):
     shape = jax.ShapeDtypeStruct((ROWS, weight.shape[1]), BF16)
     return pl.pallas_call(
         far_kernel,
-        in_specs=[HELD] * 4,
+        in_specs=[HELD] * 3,
         out_specs=[HELD] * 2,
         out_shape=[shape, shape],
         compiler_params=pltpu.CompilerParams(vmem_limit_bytes=LITTLE),
-        cost_estimate=pl.CostEstimate(flops=2 << 30, bytes_accessed=6 << 20, transcendentals=0),
+        cost_estimate=pl.CostEstimate(flops=1 << 30, bytes_accessed=5 << 20, transcendentals=0),
         name="far_product",
-    )(own, other, weight, other_weight)
-
-
-def near_kernel(flip, place_ref, own_ref, other_ref, weight_ref, other_weight_ref, *refs):
-    outs, (held, done) = refs[:2], refs[2:]
+    )(own, other, weight)
+
+
+def near_kernel(place_ref, own_ref, other_ref, weight_ref, other_weight_ref, *refs):
+    outs, (held, done) = refs[:4], refs[4:]
     columns = outs[0].shape[1]
     width = columns // 2
     steps = [(b, i) for b in range(2) for i in range(2)]
@@ -393,26 +409,27 @@
     for (b, i), pair in zip(steps, arrivals):
         for copy in pair:
             copy.wait()
-        rows = slice(ROWS, 2 * ROWS) if (b == 0) == flip else slice(0, ROWS)
-        total = jnp.dot(own_ref[rows], held[b, i, 0], preferred_element_type=F32)
-        total += jnp.dot(other_ref[rows], held[b, i, 1], preferred_element_type=F32)
-        outs[b][:, width * i : width * i + width] = total.astype(BF16)
-
-
-def near_product(own, other, out_weight, other_weight, blocks, flip):
+        lanes = slice(width * i, width * i + width)
+        total = jnp.dot(own_ref[...], held[b, i, 0], preferred_element_type=F32)
+        total += jnp.dot(other_ref[...], held[b, i, 1], preferred_element_type=F32)
+        outs[2 * b][:, lanes] = total[:ROWS].astype(BF16)
+        outs[2 * b + 1][:, lanes] = total[ROWS:].astype(BF16)
+
+
+def near_product(own, other, out_weight, other_weight, blocks):
     channels = own.shape[1]
     columns = out_weight.shape[1] // 8
     return pl.pallas_call(
-        functools.partial(near_kernel, flip),
+        near_kernel,
         in_specs=[SCALARS] + [HELD] * 2 + [FAR] * 2,
-        out_specs=[HELD] * 2,
-        out_shape=[jax.ShapeDtypeStruct((ROWS, columns), BF16)] * 2,
+        out_specs=[HELD] * 4,
+        out_shape=[jax.ShapeDtypeStruct((ROWS, columns), BF16)] * 4,
         scratch_shapes=[
             pltpu.VMEM((2, 2, 2, channels, columns // 2), BF16),
             pltpu.SemaphoreType.DMA((2, 2, 2)),
         ],
         compiler_params=pltpu.CompilerParams(vmem_limit_bytes=MOST),
-        cost_estimate=pl.CostEstimate(flops=2 << 30, bytes_accessed=10 << 20, transcendentals=0),
+        cost_estimate=pl.CostEstimate(flops=4 << 30, bytes_accessed=10 << 20, transcendentals=0),
         name="near_product",
     )(blocks, own, other, out_weight, other_weight)
 
@@ -464,16 +481,11 @@
 
 
 def finish(top, bottom, top_more, bottom_more):
-    columns = top.shape[1]
-    width = 512
-    half = pl.BlockSpec((ROWS, width), lambda i: (0, i))
     return pl.pallas_call(
         finish_kernel,
-        grid=(columns // width,),
-        in_specs=[half] * 4,
-        out_specs=pl.BlockSpec((2 * ROWS, width), lambda i: (0, i)),
-        out_shape=jax.ShapeDtypeStruct((2 * ROWS, columns), BF16),
-        compiler_params=pltpu.CompilerParams(vmem_limit_bytes=MOST),
+        in_specs=[HELD] * 4,
+        out_shape=jax.ShapeDtypeStruct((2 * ROWS, top.shape[1]), BF16),
+        compiler_params=pltpu.CompilerParams(vmem_limit_bytes=LITTLE),
         name="finish",
     )(top, bottom, top_more, bottom_more)
 
@@ -500,14 +512,15 @@
 def project(gated, out_weight, other_weight, far):
     other = core_swap(gated)
     add = lambda a, b: (a.astype(F32) + b.astype(F32)).astype(BF16)
-    far_top, far_bottom = far_product(gated, other, *far)
+    far_top, far_bottom = far_product(far_own_product(gated, far[0]), other, far[1])
     up = chip_shift(far_top, 1)
     down = chip_shift(far_bottom, -1)
     near = jnp.stack([block_of(1), block_of(3)])
-    next_bottom, last_top = near_product(gated, other, out_weight, other_weight, near, True)
+    next_top, next_bottom, last_top, last_bottom = near_product(
+        gated, other, out_weight, other_weight, near
+    )
     up_direct = chip_shift(next_bottom, 1)
     down_direct = chip_shift(last_top, -1)
-    next_top, last_bottom = near_product(gated, other, out_weight, other_weight, near, False)
     up_sum = chip_shift(add(next_top, up), 1)
     down_sum = chip_shift(add(last_bottom, down), -1)
     top, bottom = own_product(
@@ -519,16 +532,17 @@
 def convolve(key_proj, value_proj, filter_spectrum, early=()):
     first, last, forward, backward, turn, side = tables()
     as_bf16 = lambda t: jnp.asarray(t.astype(np.float32)).astype(BF16)
-    turn = jnp.asarray(turn.astype(np.float32))
-    side = jnp.asarray(side.astype(np.float32))
+    waves = np.concatenate([turn[:, :, :16], side.reshape(2, 16, 16, 128).swapaxes(0, 1)])
+    waves = jnp.asarray(waves.astype(np.float32))
+    turn = jnp.asarray(np.concatenate([turn, side[None]]).astype(np.float32))
     signal = pack_signal(key_proj, value_proj)
     signal = lax.all_to_all(signal, "ctx", split_axis=0, concat_axis=0, tiled=True)
     spectrum = pack_spectrum(filter_spectrum, as_bf16(shuffles()))
     signal, spectrum = lax.optimization_barrier((signal, spectrum))
     spectrum = lax.all_to_all(spectrum, "ctx", split_axis=0, concat_axis=0, tiled=True)
-    x = forward_part(signal, as_bf16(first), as_bf16(forward), turn, side)
+    x = forward_part(signal, as_bf16(first), as_bf16(forward), turn)
     x, *early = lax.optimization_barrier((x, *early))
-    out = filter_part(x, spectrum, as_bf16(backward), as_bf16(last), turn, side)
+    out = filter_part(x, spectrum, as_bf16(np.concatenate([backward, last])), waves)
     return lax.all_to_all(out, "ctx", split_axis=0, concat_axis=0, tiled=True), early
 
 

time: 170 us -> 165 us (0.971)
  Pallas kernels: 47.4 us -> 40.5 us
    pallas_call x7, Pallas kernels: 40.8 us -> 33.9 us  [the longest x1 9.99 us: forward_part(): pl.pallas_call(forward_kernel, in_specs=[HELD] * 4, out_specs=HELD, out_s...]
    ppermute x6, waiting for transfers between devices: 13 us -> 14.9 us  [chip_shift(): lax.ppermute(array, 'tp', [(i, (i + 2 * step) % 8) for i in range(8)])]
    unnamed x26, local copies, waits for them, and re-layouts: 5.69 us -> 7.45 us
where the time goes in v3:
time: 165 us; the launch traced here: 164 us
  waiting for transfers between devices  66.4 us (40%)
  Pallas kernels  40.5 us (25%)
  starting transfers between devices  21.3 us (13%)
  blocking collectives  18.7 us (11%)
  local copies, waits for them, and re-layouts  13.7 us (8%)
  other arithmetic  3.12 us (2%)
    all_to_all x1, waiting for transfers between devices, convolve(): lax.all_to_all(spectrum, 'ctx', split_axis=0, concat_axis=0, tiled=True)  37.4 us
    all_to_all x1, blocking collectives, convolve(): lax.all_to_all(out, 'ctx', split_axis=0, concat_axis=0, tiled=True)  18.7 us
    ppermute x6, waiting for transfers between devices, chip_shift(): lax.ppermute(array, 'tp', [(i, (i + 2 * step) % 8) for i in range(8)])  14.9 us
    all_to_all x1, waiting for transfers between devices, convolve(): lax.all_to_all(signal, 'ctx', split_axis=0, concat_axis=0, tiled=True)  12.8 us
    pallas_call x1, Pallas kernels, forward_part(): pl.pallas_call(forward_kernel, in_specs=[HELD] * 4, out_specs=HELD, out_s...  9.99 us
    ppermute x6, starting transfers between devices, chip_shift(): lax.ppermute(array, 'tp', [(i, (i + 2 * step) % 8) for i in range(8)])  8.57 us
    all_to_all x1, starting transfers between devices, convolve(): lax.all_to_all(signal, 'ctx', split_axis=0, concat_axis=0, tiled=True)  8.14 us
    pallas_call x1, Pallas kernels, near_product(): pl.pallas_call(near_kernel, in_specs=[SCALARS] + [HELD] * 2 + [FAR] * 2,...  7.93 us
  transfers between devices with their start and end apart: 10, of which 7 were waited for; matrix products, arithmetic and copies ran while one was open for 6% of the time, Pallas kernels for 17%

profile of v3, /device:TPU:0, one launch (start us, length us, event | category | flops | bytes accessed | tf_op | source)
XLA Modules:
  0.0 164.0 jit_solution(6141201009124273669)
XLA Ops:
  0.0 0.0 copy-start.11
  0.0 0.0 collective-permute-start
  0.0 3.0 %pack_signal.1 = bf16[16,256,128]{2,1,0:T(8,128)(2,1)} custom-call(bf16[512,1024]{1,0:T(8,128)(2,1)} %key_ref.3, bf16[512,1024]{1,0:T(8,128)(2,1)} %value_ref.3), custom_call_target="tpu_custom_call" | custom-call | flops 1048576 | bytes 3145728 | tf_op jit(solution)/shard_map/pack_signal/pallas_call | solution.py:98
  3.0 8.1 %all-to-all-start = ((bf16[16,256,128]{2,1,0:T(8,128)(2,1)}), bf16[16,256,128]{2,1,0:T(8,128)(2,1)S(1)}, u32[]{:S(2)}, u32[]{:S(2)}) async-start(bf16[16,256,128]{2,1,0:T(8,128)(2,1)} %pack_signal.1), calls=%async_computation | async-start | bytes 2097152 | tf_op jit(solution)/shard_map/all_to_all | solution.py:539
  11.1 0.0 copy-done.11
  11.1 0.0 copy-start.3
  11.1 2.2 %copy-done.3 = bf16[2,1024,1024]{2,1,0:T(8,128)(2,1)S(1)} copy-done((bf16[2,1024,1024]{2,1,0:T(8,128)(2,1)S(1)}, bf16[2,1024,1024]{2,1,0:T(8,128)(2,1)}, u32[]{:S(2)}) %copy-start.3) | copy-done | bytes 4194328
  13.3 1.4 pack_spectrum.1
  14.8 0.0 copy-start
  14.8 2.0 %copy-done = bf16[16,2,32,16,128]{4,3,2,1,0:T(8,128)(2,1)} copy-done((bf16[16,2,32,16,128]{4,3,2,1,0:T(8,128)(2,1)}, bf16[16,2,32,16,128]{4,3,2,1,0:T(8,128)(2,1)S(1)}, u32[]{:S(2)}) %copy-start) | copy-done | bytes 4194328
  16.8 12.8 %all-to-all-done.signal_ref = bf16[16,256,128]{2,1,0:T(8,128)(2,1)S(1)} async-done(((bf16[16,256,128]{2,1,0:T(8,128)(2,1)}), bf16[16,256,128]{2,1,0:T(8,128)(2,1)S(1)}, u32[]{:S(2)}, u32[]{:S(2)}) %all-to-all-start) | async-done | bytes 1048608 | tf_op jit(solution)/shard_map/all_to_all | solution.py:539
  29.6 4.5 %all-to-all-start.1 = ((bf16[16,2,32,16,128]{4,3,2,1,0:T(8,128)(2,1)}), bf16[16,2,32,16,128]{4,3,2,1,0:T(8,128)(2,1)}, u32[]{:S(2)}, u32[]{:S(2)}) async-start(bf16[16,2,32,16,128]{4,3,2,1,0:T(8,128)(2,1)} %copy-done), calls=%async_computation.1 | async-start | bytes 8388608 | tf_op jit(solution)/shard_map/all_to_all | solution.py:542
  34.1 0.0 copy-start.10
  34.2 3.2 %constant_dynamic-slice_fusion.1.weight_ref = bf16[1024,1024]{1,0:T(8,128)(2,1)} fusion(bf16[1024,8192]{1,0:T(8,128)(2,1)} %weight_ref.3, s32[]{:T(128)S(6)} %select_n.44), kind=kLoop, calls=%fused_computation.4 | loop fusion | bytes 4194308 | tf_op jit(solution)/shard_map/dynamic_slice | solution.py:509
  37.3 0.0 copy-done.10
  37.4 0.0 copy-start.9
  37.4 1.0 copy-done.9
  38.4 10.0 %forward_part.1.x_ref = bf16[17,2,256,128]{3,2,1,0:T(8,128)(2,1)S(1)} custom-call(bf16[512,256]{1,0:T(8,128)(2,1)S(1)} %copy-done.10, bf16[512,512]{1,0:T(8,128)(2,1)S(1)} %copy-done.9, f32[18,2,256,128]{3,2,1,0:T(8,128)} %constant.82.clone.turn_ref, bf16[16,256,128]{2,1,0:T(8,128)(2,1)S(1)} %all-to-all-done.signal_ref), custom_call_target="tpu_custom_call" | custom-call | flops 2147483648 | bytes 12582912 | tf_op jit(solution)/shard_map/forward_part/pallas_call | solution.py:200
  48.4 0.0 collective-permute-done.other_weight_ref
  48.4 3.1 %constant_dynamic-slice_fusion.weight_ref = bf16[1024,1024]{1,0:T(8,128)(2,1)} fusion(bf16[1024,8192]{1,0:T(8,128)(2,1)} %collective-permute-done.other_weight_ref, s32[]{:T(128)S(6)} %select_n.44), kind=kLoop, calls=%fused_computation.3 | loop fusion | bytes 4194308 | tf_op jit(solution)/shard_map/dynamic_slice | solution.py:509
  51.5 0.0 copy-start.4
  51.5 37.4 %all-to-all-done.1.spec_ref = bf16[16,2,32,16,128]{4,3,2,1,0:T(8,128)(2,1)} async-done(((bf16[16,2,32,16,128]{4,3,2,1,0:T(8,128)(2,1)}), bf16[16,2,32,16,128]{4,3,2,1,0:T(8,128)(2,1)}, u32[]{:S(2)}, u32[]{:S(2)}) %all-to-all-start.1) | async-done | bytes 4194336 | tf_op jit(solution)/shard_map/all_to_all | solution.py:542
  88.9 0.0 copy-start.7
  88.9 1.1 copy-done.7
  90.0 0.0 copy-start.8
  90.0 1.0 copy-done.8
  91.1 0.0 copy-start.5
  91.1 0.0 copy-start.6
  91.1 0.0 copy-start.12
  91.1 7.2 %filter_part.1 = bf16[16,256,128]{2,1,0:T(8,128)(2,1)S(1)} custom-call(bf16[768,512]{1,0:T(8,128)(2,1)S(1)} %copy-done.7, f32[33,2,16,128]{3,2,1,0:T(8,128)S(1)} %copy-done.8, bf16[17,2,256,128]{3,2,1,0:T(8,128)(2,1)S(1)} %forward_part.1.x_ref, bf16[16,2,32,16,128]{4,3,2,1,0:T(8,128)(2,1)} %all-to-all-done.1.spec_ref), custom_call_target="tpu_custom_call" | custom-call | flops 2147483648 | bytes 16777216 | tf_op jit(solution)/shard_map/filter_part/pallas_call | solution.py:306
  98.3 0.0 copy-start.1
  98.3 18.7 %all_to_all.15.filtered_ref = bf16[16,256,128]{2,1,0:T(8,128)(2,1)S(1)} all-to-all(bf16[16,256,128]{2,1,0:T(8,128)(2,1)S(1)} %filter_part.1), channel_id=1, replica_groups=mesh['ctx'=16,'tp'=8] {'ctx'}, dimensions={0} | all-to-all | bytes 2097152 | tf_op jit(solution)/shard_map/all_to_all | solution.py:546
  117.0 0.0 copy-done.4
  117.0 0.0 copy-done.5
  117.0 0.0 copy-done.6
  117.0 0.0 copy-done.12
  117.0 0.0 copy-start.2
  117.0 1.0 gate.1.own_ref
  118.0 0.1 collective-permute-start.1
  118.1 0.0 copy-done.1
  118.1 1.3 far_own_product.1.own_ref
  119.4 1.4 collective-permute-done.1.other_ref
  120.8 0.0 copy-done.2
  120.8 2.2 %far_product.1 = (bf16[256,1024]{1,0:T(8,128)(2,1)}, bf16[256,1024]{1,0:T(8,128)(2,1)}) custom-call(f32[512,1024]{1,0:T(8,128)S(1)} %far_own_product.1.own_ref, bf16[512,1024]{1,0:T(8,128)(2,1)S(1)} %collective-permute-done.1.other_ref, bf16[1024,1024]{1,0:T(8,128)(2,1)S(1)} %copy-done.2), custom_call_target="tpu_custom_call" | custom-call | flops 1073741824 | bytes 5242880 | tf_op jit(solution)/shard_map/far_product/pallas_call | solution.py:382
  122.9 1.5 collective-permute-start.4
  124.4 0.1 pad_add_fusion.place_ref
  124.5 1.7 %collective-permute-start.6 = (bf16[256,1024]{1,0:T(8,128)(2,1)}, bf16[256,1024]{1,0:T(8,128)(2,1)S(1)}, u32[]{:S(2)}, u32[]{:S(2)}) collective-permute-start(bf16[256,1024]{1,0:T(8,128)(2,1)} %get-tuple-element.30), channel_id=1, source_target_pairs={{0,6},{1,7},{2,0},{3,1},{4,2},{5,3},{6,4},{7,5},{8,14},{9,15},{10,... | collective-permute-start | bytes 1572872 | tf_op jit(solution)/shard_map/ppermute | solution.py:494
  126.2 7.9 %near_product.1 = (bf16[256,1024]{1,0:T(8,128)(2,1)S(1)}, bf16[256,1024]{1,0:T(8,128)(2,1)}, bf16[256,1024]{1,0:T(8,128)(2,1)}, bf16[256,1024]{1,0:T(8,128)(2,1)S(1)}) custom-call(s32[2]{0:T(128)S(1)} %pad_add_fusion.place_ref, bf16[512,1024]{1,0:T(8,128)(2,1)S(1)} %gate.1.own_ref, bf16[512,1024]{1,0:T(8,128)(2,1)S(1)} %collective-permute-done.1.other_ref, ...), custom_call_target="tpu_custom_call" | custom-call | flops 4294967296 | bytes 10485760 | tf_op jit(solution)/shard_map/near_product/pallas_call | solution.py:422
  134.2 1.6 collective-permute-start.2
  135.8 0.5 collective-permute-start.3
  136.3 2.1 %collective-permute-done.4 = bf16[256,1024]{1,0:T(8,128)(2,1)} collective-permute-done((bf16[256,1024]{1,0:T(8,128)(2,1)}, bf16[256,1024]{1,0:T(8,128)(2,1)}, u32[]{:S(2)}, u32[]{:S(2)}) %collective-permute-start.4) | collective-permute-done | bytes 524320 | tf_op jit(solution)/shard_map/ppermute | solution.py:494
  138.4 2.0 %add_convert_fusion.1 = bf16[256,1024]{1,0:T(8,128)(2,1)} fusion(bf16[256,1024]{1,0:T(8,128)(2,1)} %collective-permute-done.4, bf16[256,1024]{1,0:T(8,128)(2,1)S(1)} %get-tuple-element.25), kind=kLoop, calls=%fused_computation.1 | loop fusion | flops 1048576 | bytes 1572864 | tf_op jit(solution)/shard_map/convert_element_type | solution.py:514
  140.5 0.4 collective-permute-start.5
  140.9 0.0 collective-permute-done.6
  140.9 1.0 add_convert_fusion
  141.9 2.8 %collective-permute-start.7 = (bf16[256,1024]{1,0:T(8,128)(2,1)}, bf16[256,1024]{1,0:T(8,128)(2,1)}, u32[]{:S(2)}, u32[]{:S(2)}) collective-permute-start(bf16[256,1024]{1,0:T(8,128)(2,1)} %add_convert_fusion), channel_id=1, source_target_pairs={{0,6},{1,7},{2,0},{3,1},{4,2},{5,3},{6,4},{7,5},{8,14},{9,15},{10,... | collective-permute-start | bytes 1572872 | tf_op jit(solution)/shard_map/ppermute | solution.py:494
  144.7 6.0 %collective-permute-done.2.top_more_ref = bf16[256,1024]{1,0:T(8,128)(2,1)S(1)} collective-permute-done((bf16[256,1024]{1,0:T(8,128)(2,1)}, bf16[256,1024]{1,0:T(8,128)(2,1)S(1)}, u32[]{:S(2)}, u32[]{:S(2)}) %collective-permute-start.2) | collective-permute-done | bytes 524320 | tf_op jit(solution)/shard_map/ppermute | solution.py:494
  150.8 1.3 collective-permute-done.3.bottom_more_ref
  152.1 4.2 %own_product.1 = (f32[256,1024]{1,0:T(8,128)S(1)}, f32[256,1024]{1,0:T(8,128)S(1)}) custom-call(s32[1]{0:T(128)} %bitcast.place_ref, bf16[512,1024]{1,0:T(8,128)(2,1)S(1)} %gate.1.own_ref, bf16[512,1024]{1,0:T(8,128)(2,1)S(1)} %collective-permute-done.1.other_ref, bf16[1024,8192]{1,0:T(8,128)(2,1)} %weight_ref.3, ...), custom_call_target="tpu_custom_call" | custom-call | flops 2147483648 | bytes 10485760 | tf_op jit(solution)/shard_map/own_product/pallas_call | solution.py:463
  156.3 5.4 %collective-permute-done.5.top_more_ref = bf16[256,1024]{1,0:T(8,128)(2,1)} collective-permute-done((bf16[256,1024]{1,0:T(8,128)(2,1)}, bf16[256,1024]{1,0:T(8,128)(2,1)}, u32[]{:S(2)}, u32[]{:S(2)}) %collective-permute-start.5) | collective-permute-done | bytes 524320 | tf_op jit(solution)/shard_map/ppermute | solution.py:494
  161.7 0.0 collective-permute-done.7.bottom_more_ref
  161.7 2.3 %finish.1 = bf16[512,1024]{1,0:T(8,128)(2,1)} custom-call(f32[256,1024]{1,0:T(8,128)S(1)} %get-tuple-element.23.top_ref, f32[256,1024]{1,0:T(8,128)S(1)} %get-tuple-element.24.bottom_ref, bf16[256,1024]{1,0:T(8,128)(2,1)} %collective-permute-done.5.top_more_ref, bf16[256,1024]{1,0:T(8,128)(2,1)} %collective-permute-done.7.bottom_more_ref), custom_call_target="tpu_custom_call" | custom-call | tf_op jit(solution)/shard_map/finish/pallas_call | solution.py:484
Async XLA Ops:
  0.0 11.1 %copy-start.11 = (bf16[2,256,256]{2,1,0:T(8,128)(2,1)S(1)}, bf16[2,256,256]{2,1,0:T(8,128)(2,1)}, u32[]{:S(2)}) copy-start(bf16[2,256,256]{2,1,0:T(8,128)(2,1)} %constant.90.shuffle_ref) | copy-start | bytes 786436
  0.0 48.4 %collective-permute-start = (bf16[1024,8192]{1,0:T(8,128)(2,1)}, bf16[1024,8192]{1,0:T(8,128)(2,1)}, u32[]{:S(2)}, u32[]{:S(2)}) collective-permute-start(bf16[1024,8192]{1,0:T(8,128)(2,1)} %weight_ref.3), channel_id=1, source_target_pairs={{0,1},{1,0},{2,3},{3,2},{4,5},{5,4},{6,7},{7,6},{8,9},{9,8},{10,11... | collective-permute-start | bytes 50331656 | tf_op jit(solution)/shard_map/ppermute | solution.py:498
  3.0 26.6 %all-to-all-start = ((bf16[16,256,128]{2,1,0:T(8,128)(2,1)}), bf16[16,256,128]{2,1,0:T(8,128)(2,1)S(1)}, u32[]{:S(2)}, u32[]{:S(2)}) async-start(bf16[16,256,128]{2,1,0:T(8,128)(2,1)} %pack_signal.1), calls=%async_computation | async-start | bytes 2097152 | tf_op jit(solution)/shard_map/all_to_all | solution.py:539
  11.1 2.2 %copy-start.3 = (bf16[2,1024,1024]{2,1,0:T(8,128)(2,1)S(1)}, bf16[2,1024,1024]{2,1,0:T(8,128)(2,1)}, u32[]{:S(2)}) copy-start(bf16[2,1024,1024]{2,1,0:T(8,128)(2,1)} %spec_ref.1) | copy-start | bytes 12582916
  14.8 2.0 %copy-start = (bf16[16,2,32,16,128]{4,3,2,1,0:T(8,128)(2,1)}, bf16[16,2,32,16,128]{4,3,2,1,0:T(8,128)(2,1)S(1)}, u32[]{:S(2)}) copy-start(bf16[16,2,32,16,128]{4,3,2,1,0:T(8,128)(2,1)S(1)} %pack_spectrum.1) | copy-start | bytes 12582916
  29.6 59.3 %all-to-all-start.1 = ((bf16[16,2,32,16,128]{4,3,2,1,0:T(8,128)(2,1)}), bf16[16,2,32,16,128]{4,3,2,1,0:T(8,128)(2,1)}, u32[]{:S(2)}, u32[]{:S(2)}) async-start(bf16[16,2,32,16,128]{4,3,2,1,0:T(8,128)(2,1)} %copy-done), calls=%async_computation.1 | async-start | bytes 8388608 | tf_op jit(solution)/shard_map/all_to_all | solution.py:542
  34.1 3.2 %copy-start.10 = (bf16[512,256]{1,0:T(8,128)(2,1)S(1)}, bf16[512,256]{1,0:T(8,128)(2,1)}, u32[]{:S(2)}) copy-start(bf16[512,256]{1,0:T(8,128)(2,1)} %constant.88.first_ref) | copy-start | bytes 786436
  37.4 1.0 copy-start.9
  51.5 65.5 %copy-start.4 = (bf16[512,1024]{1,0:T(8,128)(2,1)S(1)}, bf16[512,1024]{1,0:T(8,128)(2,1)}, u32[]{:S(2)}) copy-start(bf16[512,1024]{1,0:T(8,128)(2,1)} %key_ref.3) | copy-start | bytes 3145732
  88.9 1.1 copy-start.7
  90.0 1.0 copy-start.8
  91.1 25.9 %copy-start.5 = (bf16[512,1024]{1,0:T(8,128)(2,1)S(1)}, bf16[512,1024]{1,0:T(8,128)(2,1)}, u32[]{:S(2)}) copy-start(bf16[512,1024]{1,0:T(8,128)(2,1)} %value_ref.3) | copy-start | bytes 3145732
  91.1 25.9 %copy-start.6 = (bf16[512,1024]{1,0:T(8,128)(2,1)S(1)}, bf16[512,1024]{1,0:T(8,128)(2,1)}, u32[]{:S(2)}) copy-start(bf16[512,1024]{1,0:T(8,128)(2,1)} %query_ref.1) | copy-start | bytes 3145732
  91.1 25.9 %copy-start.12 = (f32[1024]{0:T(1024)S(1)}, f32[1024]{0:T(1024)}, u32[]{:S(2)}) copy-start(f32[1024]{0:T(1024)} %param.16) | copy-start | bytes 12292
  98.3 19.8 %copy-start.1 = (bf16[1024,1024]{1,0:T(8,128)(2,1)S(1)}, bf16[1024,1024]{1,0:T(8,128)(2,1)}, u32[]{:S(2)}) copy-start(bf16[1024,1024]{1,0:T(8,128)(2,1)} %constant_dynamic-slice_fusion.1.weight_ref) | copy-start | bytes 6291460
  117.0 3.7 %copy-start.2 = (bf16[1024,1024]{1,0:T(8,128)(2,1)S(1)}, bf16[1024,1024]{1,0:T(8,128)(2,1)}, u32[]{:S(2)}) copy-start(bf16[1024,1024]{1,0:T(8,128)(2,1)} %constant_dynamic-slice_fusion.weight_ref) | copy-start | bytes 6291460
  118.0 2.7 %collective-permute-start.1 = (bf16[512,1024]{1,0:T(8,128)(2,1)S(1)}, bf16[512,1024]{1,0:T(8,128)(2,1)S(1)}, u32[]{:S(2)}, u32[]{:S(2)}) collective-permute-start(bf16[512,1024]{1,0:T(8,128)(2,1)S(1)} %gate.1.own_ref), channel_id=1, source_target_pairs={{0,1},{1,0},{2,3},{3,2},{4,5},{5,4},{6,7},{7,6},{8,9},{9,8},{10,11... | collective-permute-start | bytes 3145736 | tf_op jit(solution)/shard_map/ppermute | solution.py:498
  122.9 15.5 %collective-permute-start.4 = (bf16[256,1024]{1,0:T(8,128)(2,1)}, bf16[256,1024]{1,0:T(8,128)(2,1)}, u32[]{:S(2)}, u32[]{:S(2)}) collective-permute-start(bf16[256,1024]{1,0:T(8,128)(2,1)} %get-tuple-element.28), channel_id=1, source_target_pairs={{0,2},{1,3},{2,4},{3,5},{4,6},{5,7},{6,0},{7,1},{8,10},{9,11},{10,... | collective-permute-start | bytes 1572872 | tf_op jit(solution)/shard_map/ppermute | solution.py:494
  124.5 16.4 %collective-permute-start.6 = (bf16[256,1024]{1,0:T(8,128)(2,1)}, bf16[256,1024]{1,0:T(8,128)(2,1)S(1)}, u32[]{:S(2)}, u32[]{:S(2)}) collective-permute-start(bf16[256,1024]{1,0:T(8,128)(2,1)} %get-tuple-element.30), channel_id=1, source_target_pairs={{0,6},{1,7},{2,0},{3,1},{4,2},{5,3},{6,4},{7,5},{8,14},{9,15},{10,... | collective-permute-start | bytes 1572872 | tf_op jit(solution)/shard_map/ppermute | solution.py:494
  134.2 16.6 %collective-permute-start.2 = (bf16[256,1024]{1,0:T(8,128)(2,1)}, bf16[256,1024]{1,0:T(8,128)(2,1)S(1)}, u32[]{:S(2)}, u32[]{:S(2)}) collective-permute-start(bf16[256,1024]{1,0:T(8,128)(2,1)} %get-tuple-element.21), channel_id=1, source_target_pairs={{0,6},{1,7},{2,0},{3,1},{4,2},{5,3},{6,4},{7,5},{8,14},{9,15},{10,... | collective-permute-start | bytes 1572872 | tf_op jit(solution)/shard_map/ppermute | solution.py:494
  135.8 16.3 %collective-permute-start.3 = (bf16[256,1024]{1,0:T(8,128)(2,1)}, bf16[256,1024]{1,0:T(8,128)(2,1)S(1)}, u32[]{:S(2)}, u32[]{:S(2)}) collective-permute-start(bf16[256,1024]{1,0:T(8,128)(2,1)} %get-tuple-element.22), channel_id=1, source_target_pairs={{0,2},{1,3},{2,4},{3,5},{4,6},{5,7},{6,0},{7,1},{8,10},{9,11},{10,... | collective-permute-start | bytes 1572872 | tf_op jit(solution)/shard_map/ppermute | solution.py:494
  140.5 21.2 %collective-permute-start.5 = (bf16[256,1024]{1,0:T(8,128)(2,1)}, bf16[256,1024]{1,0:T(8,128)(2,1)}, u32[]{:S(2)}, u32[]{:S(2)}) collective-permute-start(bf16[256,1024]{1,0:T(8,128)(2,1)} %add_convert_fusion.1), channel_id=1, source_target_pairs={{0,2},{1,3},{2,4},{3,5},{4,6},{5,7},{6,0},{7,1},{8,10},{9,11},{10,... | collective-permute-start | bytes 1572872 | tf_op jit(solution)/shard_map/ppermute | solution.py:494
  141.9 19.8 %collective-permute-start.7 = (bf16[256,1024]{1,0:T(8,128)(2,1)}, bf16[256,1024]{1,0:T(8,128)(2,1)}, u32[]{:S(2)}, u32[]{:S(2)}) collective-permute-start(bf16[256,1024]{1,0:T(8,128)(2,1)} %add_convert_fusion), channel_id=1, source_target_pairs={{0,6},{1,7},{2,0},{3,1},{4,2},{5,3},{6,4},{7,5},{8,14},{9,15},{10,... | collective-permute-start | bytes 1572872 | tf_op jit(solution)/shard_map/ppermute | solution.py:494

commit v4 on v3

--- a/solution.py
+++ b/solution.py
@@ -475,19 +475,24 @@
     )(block, own, other, out_weight, other_weight, top_more, bottom_more)
 
 
-def finish_kernel(top_ref, bottom_ref, top_more_ref, bottom_more_ref, out_ref):
-    out_ref[:ROWS] = (top_ref[...] + top_more_ref[...].astype(F32)).astype(BF16)
-    out_ref[ROWS:] = (bottom_ref[...] + bottom_more_ref[...].astype(F32)).astype(BF16)
-
-
-def finish(top, bottom, top_more, bottom_more):
+def finish_kernel(own_ref, sum_ref, *refs):
+    refs[-1][...] = (own_ref[...] + sum_ref[...].astype(F32)).astype(BF16)
+
+
+def finish(own, summed, half, out=None):
+    rows, columns = own.shape
+    part = pl.BlockSpec((rows // 2, columns), lambda i: (i, 0))
+    given = [] if out is None else [out]
     return pl.pallas_call(
         finish_kernel,
-        in_specs=[HELD] * 4,
-        out_shape=jax.ShapeDtypeStruct((2 * ROWS, top.shape[1]), BF16),
+        grid=(2,),
+        in_specs=[part] * 2 + [pl.BlockSpec(memory_space=pl.ANY)] * len(given),
+        out_specs=pl.BlockSpec((rows // 2, columns), lambda i: (2 * half + i, 0)),
+        out_shape=jax.ShapeDtypeStruct((2 * rows, columns), BF16),
+        input_output_aliases={2: 0} if given else {},
         compiler_params=pltpu.CompilerParams(vmem_limit_bytes=LITTLE),
         name="finish",
-    )(top, bottom, top_more, bottom_more)
+    )(own, summed, *given)
 
 
 def chip_shift(array, step):
@@ -526,7 +531,8 @@
     top, bottom = own_product(
         gated, other, out_weight, other_weight, block_of(0).reshape(1), down_direct, up_direct
     )
-    return finish(top, bottom, up_sum, down_sum)
+    out = finish(bottom, down_sum, 1)
+    return finish(top, up_sum, 0, out)
 
 
 def convolve(key_proj, value_proj, filter_spectrum, early=()):

time: 165 us -> 166 us (level)
    pallas_call x1 -> x2, Pallas kernels: 2.34 us -> 3.57 us  [finish(): pl.pallas_call(finish_kernel, grid=(2,), in_specs=[part] * 2 + [pl.BlockS...]
  transfers between devices with their start and end apart: 10 -> 10, of which waited for: 7 -> 8; matrix products, arithmetic and copies ran while one was open for 6% -> 6% of each run, Pallas kernels for 17% -> 18%
where the time goes in v4:
time: 166 us; the launch traced here: 165 us
  waiting for transfers between devices  65.2 us (39%)
  Pallas kernels  41.8 us (25%)
  starting transfers between devices  22.5 us (14%)
  blocking collectives  18.7 us (11%)
  local copies, waits for them, and re-layouts  13.7 us (8%)
  other arithmetic  3.12 us (2%)
    all_to_all x1, waiting for transfers between devices, convolve(): lax.all_to_all(spectrum, 'ctx', split_axis=0, concat_axis=0, tiled=True)  37.4 us
    all_to_all x1, blocking collectives, convolve(): lax.all_to_all(out, 'ctx', split_axis=0, concat_axis=0, tiled=True)  18.7 us
    ppermute x6, waiting for transfers between devices, chip_shift(): lax.ppermute(array, 'tp', [(i, (i + 2 * step) % 8) for i in range(8)])  13.7 us
    all_to_all x1, waiting for transfers between devices, convolve(): lax.all_to_all(signal, 'ctx', split_axis=0, concat_axis=0, tiled=True)  12.8 us
    pallas_call x1, Pallas kernels, forward_part(): pl.pallas_call(forward_kernel, in_specs=[HELD] * 4, out_specs=HELD, out_s...  9.99 us
    ppermute x6, starting transfers between devices, chip_shift(): lax.ppermute(array, 'tp', [(i, (i + 2 * step) % 8) for i in range(8)])  9.75 us
    all_to_all x1, starting transfers between devices, convolve(): lax.all_to_all(signal, 'ctx', split_axis=0, concat_axis=0, tiled=True)  8.14 us
    pallas_call x1, Pallas kernels, near_product(): pl.pallas_call(near_kernel, in_specs=[SCALARS] + [HELD] * 2 + [FAR] * 2,...  7.93 us
  transfers between devices with their start and end apart: 10, of which 8 were waited for; matrix products, arithmetic and copies ran while one was open for 6% of the time, Pallas kernels for 18%

profile of v4, /device:TPU:0, one launch (start us, length us, event | category | flops | bytes accessed | tf_op | source)
XLA Modules:
  0.0 165.3 jit_solution(5995157968664060158)
XLA Ops:
  0.0 0.0 copy-start.11
  0.0 0.0 collective-permute-start
  0.0 3.0 %pack_signal.1 = bf16[16,256,128]{2,1,0:T(8,128)(2,1)} custom-call(bf16[512,1024]{1,0:T(8,128)(2,1)} %key_ref.3, bf16[512,1024]{1,0:T(8,128)(2,1)} %value_ref.3), custom_call_target="tpu_custom_call" | custom-call | flops 1048576 | bytes 3145728 | tf_op jit(solution)/shard_map/pack_signal/pallas_call | solution.py:98
  3.0 8.1 %all-to-all-start = ((bf16[16,256,128]{2,1,0:T(8,128)(2,1)}), bf16[16,256,128]{2,1,0:T(8,128)(2,1)S(1)}, u32[]{:S(2)}, u32[]{:S(2)}) async-start(bf16[16,256,128]{2,1,0:T(8,128)(2,1)} %pack_signal.1), calls=%async_computation | async-start | bytes 2097152 | tf_op jit(solution)/shard_map/all_to_all | solution.py:545
  11.1 0.0 copy-done.11
  11.1 0.0 copy-start.3
  11.1 2.2 %copy-done.3 = bf16[2,1024,1024]{2,1,0:T(8,128)(2,1)S(1)} copy-done((bf16[2,1024,1024]{2,1,0:T(8,128)(2,1)S(1)}, bf16[2,1024,1024]{2,1,0:T(8,128)(2,1)}, u32[]{:S(2)}) %copy-start.3) | copy-done | bytes 4194328
  13.3 1.4 pack_spectrum.1
  14.8 0.0 copy-start
  14.8 2.0 %copy-done = bf16[16,2,32,16,128]{4,3,2,1,0:T(8,128)(2,1)} copy-done((bf16[16,2,32,16,128]{4,3,2,1,0:T(8,128)(2,1)}, bf16[16,2,32,16,128]{4,3,2,1,0:T(8,128)(2,1)S(1)}, u32[]{:S(2)}) %copy-start) | copy-done | bytes 4194328
  16.8 12.8 %all-to-all-done.signal_ref = bf16[16,256,128]{2,1,0:T(8,128)(2,1)S(1)} async-done(((bf16[16,256,128]{2,1,0:T(8,128)(2,1)}), bf16[16,256,128]{2,1,0:T(8,128)(2,1)S(1)}, u32[]{:S(2)}, u32[]{:S(2)}) %all-to-all-start) | async-done | bytes 1048608 | tf_op jit(solution)/shard_map/all_to_all | solution.py:545
  29.6 4.5 %all-to-all-start.1 = ((bf16[16,2,32,16,128]{4,3,2,1,0:T(8,128)(2,1)}), bf16[16,2,32,16,128]{4,3,2,1,0:T(8,128)(2,1)}, u32[]{:S(2)}, u32[]{:S(2)}) async-start(bf16[16,2,32,16,128]{4,3,2,1,0:T(8,128)(2,1)} %copy-done), calls=%async_computation.1 | async-start | bytes 8388608 | tf_op jit(solution)/shard_map/all_to_all | solution.py:548
  34.1 0.0 copy-start.10
  34.2 3.2 %constant_dynamic-slice_fusion.1.weight_ref = bf16[1024,1024]{1,0:T(8,128)(2,1)} fusion(bf16[1024,8192]{1,0:T(8,128)(2,1)} %weight_ref.3, s32[]{:T(128)S(6)} %select_n.44), kind=kLoop, calls=%fused_computation.4 | loop fusion | bytes 4194308 | tf_op jit(solution)/shard_map/dynamic_slice | solution.py:514
  37.3 0.0 copy-done.10
  37.4 0.0 copy-start.9
  37.4 1.0 copy-done.9
  38.4 10.0 %forward_part.1.x_ref = bf16[17,2,256,128]{3,2,1,0:T(8,128)(2,1)S(1)} custom-call(bf16[512,256]{1,0:T(8,128)(2,1)S(1)} %copy-done.10, bf16[512,512]{1,0:T(8,128)(2,1)S(1)} %copy-done.9, f32[18,2,256,128]{3,2,1,0:T(8,128)} %constant.82.clone.turn_ref, bf16[16,256,128]{2,1,0:T(8,128)(2,1)S(1)} %all-to-all-done.signal_ref), custom_call_target="tpu_custom_call" | custom-call | flops 2147483648 | bytes 12582912 | tf_op jit(solution)/shard_map/forward_part/pallas_call | solution.py:200
  48.4 0.0 collective-permute-done.other_weight_ref
  48.4 3.1 %constant_dynamic-slice_fusion.weight_ref = bf16[1024,1024]{1,0:T(8,128)(2,1)} fusion(bf16[1024,8192]{1,0:T(8,128)(2,1)} %collective-permute-done.other_weight_ref, s32[]{:T(128)S(6)} %select_n.44), kind=kLoop, calls=%fused_computation.3 | loop fusion | bytes 4194308 | tf_op jit(solution)/shard_map/dynamic_slice | solution.py:514
  51.5 0.0 copy-start.4
  51.5 37.4 %all-to-all-done.1.spec_ref = bf16[16,2,32,16,128]{4,3,2,1,0:T(8,128)(2,1)} async-done(((bf16[16,2,32,16,128]{4,3,2,1,0:T(8,128)(2,1)}), bf16[16,2,32,16,128]{4,3,2,1,0:T(8,128)(2,1)}, u32[]{:S(2)}, u32[]{:S(2)}) %all-to-all-start.1) | async-done | bytes 4194336 | tf_op jit(solution)/shard_map/all_to_all | solution.py:548
  88.9 0.0 copy-start.7
  88.9 1.1 copy-done.7
  90.0 0.0 copy-start.8
  90.0 1.0 copy-done.8
  91.1 0.0 copy-start.5
  91.1 0.0 copy-start.6
  91.1 0.0 copy-start.12
  91.1 7.2 %filter_part.1 = bf16[16,256,128]{2,1,0:T(8,128)(2,1)S(1)} custom-call(bf16[768,512]{1,0:T(8,128)(2,1)S(1)} %copy-done.7, f32[33,2,16,128]{3,2,1,0:T(8,128)S(1)} %copy-done.8, bf16[17,2,256,128]{3,2,1,0:T(8,128)(2,1)S(1)} %forward_part.1.x_ref, bf16[16,2,32,16,128]{4,3,2,1,0:T(8,128)(2,1)} %all-to-all-done.1.spec_ref), custom_call_target="tpu_custom_call" | custom-call | flops 2147483648 | bytes 16777216 | tf_op jit(solution)/shard_map/filter_part/pallas_call | solution.py:306
  98.3 0.0 copy-start.1
  98.3 18.7 %all_to_all.15.filtered_ref = bf16[16,256,128]{2,1,0:T(8,128)(2,1)S(1)} all-to-all(bf16[16,256,128]{2,1,0:T(8,128)(2,1)S(1)} %filter_part.1), channel_id=1, replica_groups=mesh['ctx'=16,'tp'=8] {'ctx'}, dimensions={0} | all-to-all | bytes 2097152 | tf_op jit(solution)/shard_map/all_to_all | solution.py:552
  117.0 0.0 copy-done.4
  117.0 0.0 copy-done.5
  117.0 0.0 copy-done.6
  117.0 0.0 copy-done.12
  117.0 0.0 copy-start.2
  117.0 1.0 gate.1.own_ref
  118.0 0.1 collective-permute-start.1
  118.1 0.0 copy-done.1
  118.1 1.3 far_own_product.1.own_ref
  119.4 1.4 collective-permute-done.1.other_ref
  120.8 0.0 copy-done.2
  120.8 2.2 %far_product.1 = (bf16[256,1024]{1,0:T(8,128)(2,1)}, bf16[256,1024]{1,0:T(8,128)(2,1)}) custom-call(f32[512,1024]{1,0:T(8,128)S(1)} %far_own_product.1.own_ref, bf16[512,1024]{1,0:T(8,128)(2,1)S(1)} %collective-permute-done.1.other_ref, bf16[1024,1024]{1,0:T(8,128)(2,1)S(1)} %copy-done.2), custom_call_target="tpu_custom_call" | custom-call | flops 1073741824 | bytes 5242880 | tf_op jit(solution)/shard_map/far_product/pallas_call | solution.py:382
  123.0 2.8 %collective-permute-start.6 = (bf16[256,1024]{1,0:T(8,128)(2,1)}, bf16[256,1024]{1,0:T(8,128)(2,1)}, u32[]{:S(2)}, u32[]{:S(2)}) collective-permute-start(bf16[256,1024]{1,0:T(8,128)(2,1)} %get-tuple-element.30), channel_id=1, source_target_pairs={{0,6},{1,7},{2,0},{3,1},{4,2},{5,3},{6,4},{7,5},{8,14},{9,15},{10,... | collective-permute-start | bytes 1572872 | tf_op jit(solution)/shard_map/ppermute | solution.py:499
  125.7 0.1 pad_add_fusion.place_ref
  125.8 0.0 collective-permute-start.4
  125.8 7.9 %near_product.1 = (bf16[256,1024]{1,0:T(8,128)(2,1)S(1)}, bf16[256,1024]{1,0:T(8,128)(2,1)}, bf16[256,1024]{1,0:T(8,128)(2,1)}, bf16[256,1024]{1,0:T(8,128)(2,1)S(1)}) custom-call(s32[2]{0:T(128)S(1)} %pad_add_fusion.place_ref, bf16[512,1024]{1,0:T(8,128)(2,1)S(1)} %gate.1.own_ref, bf16[512,1024]{1,0:T(8,128)(2,1)S(1)} %collective-permute-done.1.other_ref, ...), custom_call_target="tpu_custom_call" | custom-call | flops 4294967296 | bytes 10485760 | tf_op jit(solution)/shard_map/near_product/pallas_call | solution.py:422
  133.7 3.3 %collective-permute-start.2 = (bf16[256,1024]{1,0:T(8,128)(2,1)}, bf16[256,1024]{1,0:T(8,128)(2,1)S(1)}, u32[]{:S(2)}, u32[]{:S(2)}) collective-permute-start(bf16[256,1024]{1,0:T(8,128)(2,1)} %get-tuple-element.21), channel_id=1, source_target_pairs={{0,6},{1,7},{2,0},{3,1},{4,2},{5,3},{6,4},{7,5},{8,14},{9,15},{10,... | collective-permute-start | bytes 1572872 | tf_op jit(solution)/shard_map/ppermute | solution.py:499
  137.0 0.0 collective-permute-start.3
  137.0 0.9 collective-permute-done.6
  137.9 2.0 %add_convert_fusion = bf16[256,1024]{1,0:T(8,128)(2,1)} fusion(bf16[256,1024]{1,0:T(8,128)(2,1)} %collective-permute-done.6, bf16[256,1024]{1,0:T(8,128)(2,1)S(1)} %get-tuple-element.29), kind=kLoop, calls=%fused_computation | loop fusion | flops 1048576 | bytes 1572864 | tf_op jit(solution)/shard_map/convert_element_type | solution.py:519
  140.0 3.7 %collective-permute-start.7 = (bf16[256,1024]{1,0:T(8,128)(2,1)}, bf16[256,1024]{1,0:T(8,128)(2,1)}, u32[]{:S(2)}, u32[]{:S(2)}) collective-permute-start(bf16[256,1024]{1,0:T(8,128)(2,1)} %add_convert_fusion), channel_id=1, source_target_pairs={{0,6},{1,7},{2,0},{3,1},{4,2},{5,3},{6,4},{7,5},{8,14},{9,15},{10,... | collective-permute-start | bytes 1572872 | tf_op jit(solution)/shard_map/ppermute | solution.py:499
  143.7 0.0 collective-permute-done.4
  143.7 1.0 add_convert_fusion.1
  144.7 0.0 collective-permute-start.5
  144.7 5.0 %collective-permute-done.2.top_more_ref = bf16[256,1024]{1,0:T(8,128)(2,1)S(1)} collective-permute-done((bf16[256,1024]{1,0:T(8,128)(2,1)}, bf16[256,1024]{1,0:T(8,128)(2,1)S(1)}, u32[]{:S(2)}, u32[]{:S(2)}) %collective-permute-start.2) | collective-permute-done | bytes 524320 | tf_op jit(solution)/shard_map/ppermute | solution.py:499
  149.7 3.6 %collective-permute-done.3.bottom_more_ref = bf16[256,1024]{1,0:T(8,128)(2,1)S(1)} collective-permute-done((bf16[256,1024]{1,0:T(8,128)(2,1)}, bf16[256,1024]{1,0:T(8,128)(2,1)S(1)}, u32[]{:S(2)}, u32[]{:S(2)}) %collective-permute-start.3) | collective-permute-done | bytes 524320 | tf_op jit(solution)/shard_map/ppermute | solution.py:499
  153.3 4.2 %own_product.1 = (f32[256,1024]{1,0:T(8,128)S(1)}, f32[256,1024]{1,0:T(8,128)S(1)}) custom-call(s32[1]{0:T(128)} %bitcast.place_ref, bf16[512,1024]{1,0:T(8,128)(2,1)S(1)} %gate.1.own_ref, bf16[512,1024]{1,0:T(8,128)(2,1)S(1)} %collective-permute-done.1.other_ref, bf16[1024,8192]{1,0:T(8,128)(2,1)} %weight_ref.3, ...), custom_call_target="tpu_custom_call" | custom-call | flops 2147483648 | bytes 10485760 | tf_op jit(solution)/shard_map/own_product/pallas_call | solution.py:463
  157.6 2.4 %collective-permute-done.7.sum_ref = bf16[256,1024]{1,0:T(8,128)(2,1)} collective-permute-done((bf16[256,1024]{1,0:T(8,128)(2,1)}, bf16[256,1024]{1,0:T(8,128)(2,1)}, u32[]{:S(2)}, u32[]{:S(2)}) %collective-permute-start.7) | collective-permute-done | bytes 524320 | tf_op jit(solution)/shard_map/ppermute | solution.py:499
  160.0 1.8 %finish.2.refs_0_ = bf16[512,1024]{1,0:T(8,128)(2,1)} custom-call(f32[256,1024]{1,0:T(8,128)S(1)} %get-tuple-element.28.own_ref, bf16[256,1024]{1,0:T(8,128)(2,1)} %collective-permute-done.7.sum_ref), custom_call_target="tpu_custom_call" | custom-call | tf_op jit(solution)/shard_map/finish/pallas_call | solution.py:486
  161.8 1.7 %collective-permute-done.5.sum_ref = bf16[256,1024]{1,0:T(8,128)(2,1)} collective-permute-done((bf16[256,1024]{1,0:T(8,128)(2,1)}, bf16[256,1024]{1,0:T(8,128)(2,1)}, u32[]{:S(2)}, u32[]{:S(2)}) %collective-permute-start.5) | collective-permute-done | bytes 524320 | tf_op jit(solution)/shard_map/ppermute | solution.py:499
  163.5 1.8 %finish.3 = bf16[512,1024]{1,0:T(8,128)(2,1)} custom-call(f32[256,1024]{1,0:T(8,128)S(1)} %get-tuple-element.23.own_ref, bf16[256,1024]{1,0:T(8,128)(2,1)} %collective-permute-done.5.sum_ref, bf16[512,1024]{1,0:T(8,128)(2,1)} %finish.2.refs_0_), custom_call_target="tpu_custom_call", output_to_operand_aliasing={{}: (2, {})} | custom-call | tf_op jit(solution)/shard_map/finish/pallas_call | solution.py:486
Async XLA Ops:
  0.0 11.1 %copy-start.11 = (bf16[2,256,256]{2,1,0:T(8,128)(2,1)S(1)}, bf16[2,256,256]{2,1,0:T(8,128)(2,1)}, u32[]{:S(2)}) copy-start(bf16[2,256,256]{2,1,0:T(8,128)(2,1)} %constant.90.shuffle_ref) | copy-start | bytes 786436
  0.0 48.4 %collective-permute-start = (bf16[1024,8192]{1,0:T(8,128)(2,1)}, bf16[1024,8192]{1,0:T(8,128)(2,1)}, u32[]{:S(2)}, u32[]{:S(2)}) collective-permute-start(bf16[1024,8192]{1,0:T(8,128)(2,1)} %weight_ref.3), channel_id=1, source_target_pairs={{0,1},{1,0},{2,3},{3,2},{4,5},{5,4},{6,7},{7,6},{8,9},{9,8},{10,11... | collective-permute-start | bytes 50331656 | tf_op jit(solution)/shard_map/ppermute | solution.py:503
  3.0 26.6 %all-to-all-start = ((bf16[16,256,128]{2,1,0:T(8,128)(2,1)}), bf16[16,256,128]{2,1,0:T(8,128)(2,1)S(1)}, u32[]{:S(2)}, u32[]{:S(2)}) async-start(bf16[16,256,128]{2,1,0:T(8,128)(2,1)} %pack_signal.1), calls=%async_computation | async-start | bytes 2097152 | tf_op jit(solution)/shard_map/all_to_all | solution.py:545
  11.1 2.2 %copy-start.3 = (bf16[2,1024,1024]{2,1,0:T(8,128)(2,1)S(1)}, bf16[2,1024,1024]{2,1,0:T(8,128)(2,1)}, u32[]{:S(2)}) copy-start(bf16[2,1024,1024]{2,1,0:T(8,128)(2,1)} %spec_ref.1) | copy-start | bytes 12582916
  14.8 2.0 %copy-start = (bf16[16,2,32,16,128]{4,3,2,1,0:T(8,128)(2,1)}, bf16[16,2,32,16,128]{4,3,2,1,0:T(8,128)(2,1)S(1)}, u32[]{:S(2)}) copy-start(bf16[16,2,32,16,128]{4,3,2,1,0:T(8,128)(2,1)S(1)} %pack_spectrum.1) | copy-start | bytes 12582916
  29.6 59.3 %all-to-all-start.1 = ((bf16[16,2,32,16,128]{4,3,2,1,0:T(8,128)(2,1)}), bf16[16,2,32,16,128]{4,3,2,1,0:T(8,128)(2,1)}, u32[]{:S(2)}, u32[]{:S(2)}) async-start(bf16[16,2,32,16,128]{4,3,2,1,0:T(8,128)(2,1)} %copy-done), calls=%async_computation.1 | async-start | bytes 8388608 | tf_op jit(solution)/shard_map/all_to_all | solution.py:548
  34.1 3.2 %copy-start.10 = (bf16[512,256]{1,0:T(8,128)(2,1)S(1)}, bf16[512,256]{1,0:T(8,128)(2,1)}, u32[]{:S(2)}) copy-start(bf16[512,256]{1,0:T(8,128)(2,1)} %constant.88.first_ref) | copy-start | bytes 786436
  37.4 1.0 copy-start.9
  51.5 65.5 %copy-start.4 = (bf16[512,1024]{1,0:T(8,128)(2,1)S(1)}, bf16[512,1024]{1,0:T(8,128)(2,1)}, u32[]{:S(2)}) copy-start(bf16[512,1024]{1,0:T(8,128)(2,1)} %key_ref.3) | copy-start | bytes 3145732
  88.9 1.1 copy-start.7
  90.0 1.0 copy-start.8
  91.1 25.9 %copy-start.5 = (bf16[512,1024]{1,0:T(8,128)(2,1)S(1)}, bf16[512,1024]{1,0:T(8,128)(2,1)}, u32[]{:S(2)}) copy-start(bf16[512,1024]{1,0:T(8,128)(2,1)} %value_ref.3) | copy-start | bytes 3145732
  91.1 25.9 %copy-start.6 = (bf16[512,1024]{1,0:T(8,128)(2,1)S(1)}, bf16[512,1024]{1,0:T(8,128)(2,1)}, u32[]{:S(2)}) copy-start(bf16[512,1024]{1,0:T(8,128)(2,1)} %query_ref.1) | copy-start | bytes 3145732
  91.1 25.9 %copy-start.12 = (f32[1024]{0:T(1024)S(1)}, f32[1024]{0:T(1024)}, u32[]{:S(2)}) copy-start(f32[1024]{0:T(1024)} %param.16) | copy-start | bytes 12292
  98.3 19.8 %copy-start.1 = (bf16[1024,1024]{1,0:T(8,128)(2,1)S(1)}, bf16[1024,1024]{1,0:T(8,128)(2,1)}, u32[]{:S(2)}) copy-start(bf16[1024,1024]{1,0:T(8,128)(2,1)} %constant_dynamic-slice_fusion.1.weight_ref) | copy-start | bytes 6291460
  117.0 3.7 %copy-start.2 = (bf16[1024,1024]{1,0:T(8,128)(2,1)S(1)}, bf16[1024,1024]{1,0:T(8,128)(2,1)}, u32[]{:S(2)}) copy-start(bf16[1024,1024]{1,0:T(8,128)(2,1)} %constant_dynamic-slice_fusion.weight_ref) | copy-start | bytes 6291460
  118.0 2.7 %collective-permute-start.1 = (bf16[512,1024]{1,0:T(8,128)(2,1)S(1)}, bf16[512,1024]{1,0:T(8,128)(2,1)S(1)}, u32[]{:S(2)}, u32[]{:S(2)}) collective-permute-start(bf16[512,1024]{1,0:T(8,128)(2,1)S(1)} %gate.1.own_ref), channel_id=1, source_target_pairs={{0,1},{1,0},{2,3},{3,2},{4,5},{5,4},{6,7},{7,6},{8,9},{9,8},{10,11... | collective-permute-start | bytes 3145736 | tf_op jit(solution)/shard_map/ppermute | solution.py:503
  123.0 15.0 %collective-permute-start.6 = (bf16[256,1024]{1,0:T(8,128)(2,1)}, bf16[256,1024]{1,0:T(8,128)(2,1)}, u32[]{:S(2)}, u32[]{:S(2)}) collective-permute-start(bf16[256,1024]{1,0:T(8,128)(2,1)} %get-tuple-element.30), channel_id=1, source_target_pairs={{0,6},{1,7},{2,0},{3,1},{4,2},{5,3},{6,4},{7,5},{8,14},{9,15},{10,... | collective-permute-start | bytes 1572872 | tf_op jit(solution)/shard_map/ppermute | solution.py:499
  125.8 17.9 %collective-permute-start.4 = (bf16[256,1024]{1,0:T(8,128)(2,1)}, bf16[256,1024]{1,0:T(8,128)(2,1)S(1)}, u32[]{:S(2)}, u32[]{:S(2)}) collective-permute-start(bf16[256,1024]{1,0:T(8,128)(2,1)} %get-tuple-element.27), channel_id=1, source_target_pairs={{0,2},{1,3},{2,4},{3,5},{4,6},{5,7},{6,0},{7,1},{8,10},{9,11},{10,... | collective-permute-start | bytes 1572872 | tf_op jit(solution)/shard_map/ppermute | solution.py:499
  133.7 16.0 %collective-permute-start.2 = (bf16[256,1024]{1,0:T(8,128)(2,1)}, bf16[256,1024]{1,0:T(8,128)(2,1)S(1)}, u32[]{:S(2)}, u32[]{:S(2)}) collective-permute-start(bf16[256,1024]{1,0:T(8,128)(2,1)} %get-tuple-element.21), channel_id=1, source_target_pairs={{0,6},{1,7},{2,0},{3,1},{4,2},{5,3},{6,4},{7,5},{8,14},{9,15},{10,... | collective-permute-start | bytes 1572872 | tf_op jit(solution)/shard_map/ppermute | solution.py:499
  137.0 16.3 %collective-permute-start.3 = (bf16[256,1024]{1,0:T(8,128)(2,1)}, bf16[256,1024]{1,0:T(8,128)(2,1)S(1)}, u32[]{:S(2)}, u32[]{:S(2)}) collective-permute-start(bf16[256,1024]{1,0:T(8,128)(2,1)} %get-tuple-element.22), channel_id=1, source_target_pairs={{0,2},{1,3},{2,4},{3,5},{4,6},{5,7},{6,0},{7,1},{8,10},{9,11},{10,... | collective-permute-start | bytes 1572872 | tf_op jit(solution)/shard_map/ppermute | solution.py:499
  140.0 20.0 %collective-permute-start.7 = (bf16[256,1024]{1,0:T(8,128)(2,1)}, bf16[256,1024]{1,0:T(8,128)(2,1)}, u32[]{:S(2)}, u32[]{:S(2)}) collective-permute-start(bf16[256,1024]{1,0:T(8,128)(2,1)} %add_convert_fusion), channel_id=1, source_target_pairs={{0,6},{1,7},{2,0},{3,1},{4,2},{5,3},{6,4},{7,5},{8,14},{9,15},{10,... | collective-permute-start | bytes 1572872 | tf_op jit(solution)/shard_map/ppermute | solution.py:499
  144.7 18.8 %collective-permute-start.5 = (bf16[256,1024]{1,0:T(8,128)(2,1)}, bf16[256,1024]{1,0:T(8,128)(2,1)}, u32[]{:S(2)}, u32[]{:S(2)}) collective-permute-start(bf16[256,1024]{1,0:T(8,128)(2,1)} %add_convert_fusion.1), channel_id=1, source_target_pairs={{0,2},{1,3},{2,4},{3,5},{4,6},{5,7},{6,0},{7,1},{8,10},{9,11},{10,... | collective-permute-start | bytes 1572872 | tf_op jit(solution)/shard_map/ppermute | solution.py:499
